TPU v7x, 32 devices: a whole 2x2x4 slice. The times are simulated.
32 devices in a mesh: row: 4 (over x, core), col: 8 (over z, y).
Axes of the slice: x: 2, y: 2, z: 4, core: 2. Of those that a mesh axis runs over, the one named last changes fastest.
Arguments:
- front_blocks: float32 [32, 512, 16, 1024], P(None, 'row', None, 'col'), may hold values from -2.5 to 10.5, as said below
- child_updates: bfloat16 [2, 24, 512, 12, 1024], P(None, None, 'row', None, 'col'), may hold values from -0.2 to 2.2, as said below
- child_map: int32 [2, 96], replicated, may hold values from 0 to 127, as said below
Outputs:
- factored: float32 [32, 512, 16, 1024], P(None, 'row', None, 'col')
Inputs may be any that keep to these rules, and one draw needn't show every extreme that they name: `child_map`: for each child, block a * 8 + j (0 <= j < 8) lands in front block h_a * 8 + ((s_a - j) mod 8), with 12 distinct h_a below 16 and s_a = (s + q_a) mod 8, q a permutation of 0 .. 11. Hence along col one device sends at most 2 of a child's column blocks to one device, along row at most 6 of its row blocks, and both bounds are reached in every draw. `front_blocks`: symmetric positive definite. `child_updates`: each child update is symmetric.
All inputs are finite; a program needn't handle non-finite values.
Results may differ from a plain program's by a relative error of at most 0.0003.
Values may be sent and summed in bfloat16 or wider, within the bound.
No kernel may reach another device: no remote copies, remote signals or barrier semaphores. Data moves between devices by JAX's collectives and lax.ppermute only.
A program may use at most 256 MiB of HBM per device.

v0:
```python
import jax
import jax.numpy as jnp
from jax import lax
from jax.sharding import PartitionSpec as P

PW = 256
PANELS = 2
PD = 512


def spread_2(value, axis, source):
    kept = jnp.where(lax.axis_index(axis) == source, value, 0).astype(value.dtype)
    return lax.psum(kept, axis)


def earlier_count(targets):
    count_all = targets.shape[1]
    matches = targets[:, :, None, :] == targets[:, None, :, :]
    order_ids = jnp.arange(count_all)
    before = (order_ids[None, :] < order_ids[:, None])[None, :, :, None]
    return jnp.sum(matches & before, axis=2)


def arrival_info(block_map, my_index, devices):
    child_count = block_map.shape[0]
    slot_total = block_map.shape[1] // devices
    block_grid = block_map.reshape(child_count, slot_total, devices)
    targets = block_grid % devices
    home_slots = block_grid // devices
    arriving = targets == my_index
    arrival_flat = arriving.reshape(child_count, slot_total * devices).astype(jnp.int32)
    positions = (jnp.cumsum(arrival_flat, axis=1) - 1).reshape(child_count, slot_total, devices)
    return (targets, home_slots, arriving, positions)


def route_tables(block_map, my_index, devices, capacity, slot_count):
    child_count = block_map.shape[0]
    slot_total = block_map.shape[1] // devices
    targets, home_slots, arriving, positions = arrival_info(block_map, my_index, devices)
    slot_ranks = earlier_count(targets)
    my_targets = lax.dynamic_index_in_dim(targets, my_index, axis=2, keepdims=False)
    my_ranks = lax.dynamic_index_in_dim(slot_ranks, my_index, axis=2, keepdims=False)
    child_ids = jnp.arange(child_count)[:, None]
    slot_values = jnp.broadcast_to(
        jnp.arange(slot_total, dtype=jnp.int32)[None, :], (child_count, slot_total)
    )
    send_index = jnp.full((child_count, devices * capacity), slot_total, jnp.int32)
    send_index = send_index.at[child_ids, my_targets * capacity + my_ranks].set(slot_values)
    sources = jnp.arange(devices, dtype=jnp.int32)[None, None, :]
    where_from = jnp.where(arriving, sources * capacity + slot_ranks, devices * capacity)
    where_to = jnp.where(arriving, home_slots, slot_count)
    place_index = jnp.full((child_count, slot_count + 1), devices * capacity, jnp.int32)
    place_index = place_index.at[child_ids[:, :, None], where_to].set(where_from)
    return (send_index, place_index[:, :slot_count])


def pick_slots(payload, index_table, axis_no):
    return jax.vmap(lambda part_data, part_index: jnp.take(part_data, part_index, axis=axis_no))(
        payload, index_table
    )


def move_rows(payload, block_map, slot_count):
    devices = lax.axis_size("row")
    my_index = lax.axis_index("row")
    col_devices = lax.axis_size("col")
    child_count, slot_total, tile_size, row_width = payload.shape
    col_slots = block_map.shape[1] // col_devices
    capacity = col_devices // devices * ((col_slots + devices - 1) // devices)
    send_index, place_index = route_tables(block_map, my_index, devices, capacity, slot_count)
    padded = jnp.concatenate(
        [payload, jnp.zeros((child_count, 1, tile_size, row_width), payload.dtype)], axis=1
    )
    outgoing = pick_slots(padded, send_index, 0).reshape(
        child_count, devices * capacity * tile_size, row_width
    )
    incoming = lax.all_to_all(outgoing, "row", split_axis=1, concat_axis=1, tiled=True)
    incoming = incoming.reshape(child_count, devices * capacity, tile_size, row_width)
    padded_in = jnp.concatenate(
        [incoming, jnp.zeros((child_count, 1, tile_size, row_width), incoming.dtype)], axis=1
    )
    return pick_slots(padded_in, place_index, 0)


def move_columns(payload, block_map, slot_count):
    devices = lax.axis_size("col")
    my_index = lax.axis_index("col")
    child_count, height, slot_total, tile_size = payload.shape
    capacity = (slot_total + devices - 1) // devices
    send_index, place_index = route_tables(block_map, my_index, devices, capacity, slot_count)
    padded = jnp.concatenate(
        [payload, jnp.zeros((child_count, height, 1, tile_size), payload.dtype)], axis=2
    )
    outgoing = pick_slots(padded, send_index, 1).reshape(
        child_count, height, devices * capacity * tile_size
    )
    incoming = lax.all_to_all(outgoing, "col", split_axis=2, concat_axis=2, tiled=True)
    incoming = incoming.reshape(child_count, height, devices * capacity, tile_size)
    padded_in = jnp.concatenate(
        [incoming, jnp.zeros((child_count, height, 1, tile_size), incoming.dtype)], axis=2
    )
    return pick_slots(padded_in, place_index, 1)


def on_device(front_blocks, child_updates, child_map):
    row_count = lax.axis_size("row")
    col_count = lax.axis_size("col")
    row_index = lax.axis_index("row")
    col_index = lax.axis_index("col")
    front_slots_r = front_blocks.shape[0]
    tile_size = front_blocks.shape[1]
    front_slots_c = front_blocks.shape[2]
    child_count = child_updates.shape[0]
    child_rows = child_updates.shape[1]
    child_cols = child_updates.shape[3]
    arrived = move_rows(
        child_updates.reshape(child_count, child_rows, tile_size, child_cols * tile_size),
        child_map,
        front_slots_r,
    )
    arrived = move_columns(
        arrived.reshape(child_count, front_slots_r * tile_size, child_cols, tile_size),
        child_map,
        front_slots_c,
    )
    height = front_slots_r * tile_size
    breadth = front_slots_c * tile_size
    children_sum = jnp.sum(arrived.astype(jnp.float32), axis=0).reshape(height, breadth)
    assembled = front_blocks.reshape(height, breadth) + children_sum
    local_rows = jnp.arange(height, dtype=jnp.int32)
    row_global = (
        local_rows // tile_size * row_count + row_index
    ) * tile_size + local_rows % tile_size
    local_cols = jnp.arange(breadth, dtype=jnp.int32)
    col_global = (
        local_cols // tile_size * col_count + col_index
    ) * tile_size + local_cols % tile_size
    panel_tiles = PW // tile_size
    spread = col_count // row_count
    row_factors = []
    col_factors = []
    for panel_no in range(PANELS):
        first_col = panel_no * PW
        finish = first_col + PW
        column_tiles = []
        for tile_no in range(panel_tiles):
            global_tile = panel_no * panel_tiles + tile_no
            col_slot = global_tile // col_count
            column_tile = assembled[:, col_slot * tile_size : (col_slot + 1) * tile_size]
            column_tiles.append(column_tile)
        pieces = [
            jnp.where(
                col_index == (panel_no * panel_tiles + tile_no) % col_count,
                column_tiles[tile_no],
                0.0,
            )
            for tile_no in range(panel_tiles)
        ]
        panel_rows = lax.psum(jnp.concatenate(pieces, axis=1), "col")
        diag_pieces = []
        for tile_no in range(panel_tiles):
            global_tile = panel_no * panel_tiles + tile_no
            row_slot = global_tile // row_count
            diag_pieces.append(
                jnp.where(
                    row_index == global_tile % row_count,
                    panel_rows[row_slot * tile_size : (row_slot + 1) * tile_size],
                    0.0,
                )
            )
        diagonal = lax.psum(jnp.concatenate(diag_pieces, axis=0), "row")
        factor = jnp.linalg.cholesky(diagonal)
        solved = lax.linalg.triangular_solve(
            factor, panel_rows, left_side=False, lower=True, transpose_a=True
        )
        lower_part = jnp.where(row_global[:, None] >= finish, solved, 0.0)
        inside = (row_global >= first_col) & (row_global < finish)
        factor_rows = jnp.take(factor, jnp.clip(row_global - first_col, 0, PW - 1), axis=0)
        lower_part = jnp.where(inside[:, None], factor_rows, lower_part)
        chosen = lax.dynamic_index_in_dim(
            lower_part.reshape(front_slots_c, spread, tile_size, PW),
            col_index // row_count,
            axis=1,
            keepdims=False,
        ).reshape(breadth, PW)
        col_part = spread_2(chosen, "row", col_index % row_count)
        assembled = assembled - jnp.dot(
            lower_part,
            col_part.T,
            precision=lax.Precision.HIGHEST,
            preferred_element_type=jnp.float32,
        )
        row_factors.append(lower_part)
        col_factors.append(col_part)
    result = assembled
    for panel_no in range(PANELS):
        for tile_no in range(panel_tiles):
            global_tile = panel_no * panel_tiles + tile_no
            col_slot = global_tile // col_count
            owner_here = col_index == global_tile % col_count
            current = result[:, col_slot * tile_size : (col_slot + 1) * tile_size]
            fresh = row_factors[panel_no][:, tile_no * tile_size : (tile_no + 1) * tile_size]
            result = result.at[:, col_slot * tile_size : (col_slot + 1) * tile_size].set(
                jnp.where(owner_here, fresh, current)
            )
    upper_mask = (row_global[:, None] < PD) & (col_global[None, :] >= PD)
    result = jnp.where(upper_mask, 0.0, result)
    return result.reshape(front_slots_r, tile_size, front_slots_c, tile_size)


def solution(mesh):
    placed = (P(None, "row", None, "col"), P(None, None, "row", None, "col"), P())
    return jax.shard_map(
        on_device,
        mesh=mesh,
        in_specs=placed,
        out_specs=P(None, "row", None, "col"),
        check_vma=False,
    )
```

profile of v0, /device:TPU:0, one launch (start us, length us, event | category | flops | bytes accessed | tf_op | source)
XLA Modules:
  0.0 2431.7 jit_solution(5047274929488769050)
XLA Ops:
  10.8 24.6 %copy.71 = bf16[2,24,128,12,128]{2,4,3,1,0:T(8,128)(2,1)} copy(bf16[2,24,128,12,128]{4,2,3,1,0:T(8,128)(2,1)} %param.17) | data formatting | bytes 37748736 | tf_op args[1]
  67.0 24.6 %copy.73 = bf16[48,128,1536]{2,1,0:T(8,128)(2,1)} copy(bf16[48,128,1536]{1,2,0:T(8,128)(2,1)} %gather_fusion) | data formatting | bytes 37748736 | tf_op jit(solution)/shard_map/vmap(jit(_take))/gather | solution.py:58
  101.6 103.4 %copy.74 = bf16[2,3072,1536]{2,0,1:T(2,128)(2,1)} copy(bf16[2,3072,1536]{2,1,0:T(8,128)(2,1)S(1)} %bitcast_select_fusion.1) | data formatting | bytes 37748736 | tf_op jit(solution)/shard_map/vmap(jit(_take))/select_n | solution.py:58
  236.3 182.5 %all-to-all-done = bf16[2,3072,1536]{2,0,1:T(2,128)(2,1)} async-done(((bf16[2,3072,1536]{2,0,1:T(2,128)(2,1)}), bf16[2,3072,1536]{2,0,1:T(2,128)(2,1)}, u32[]{:S(2)}, u32[]{:S(2)}) %all-to-all-start) | async-done | bytes 18874400 | tf_op jit(solution)/shard_map/all_to_all | solution.py:77
  455.9 45.0 %reshape.736 = bf16[2,4096,12,128]{3,2,1,0:T(8,128)(2,1)} reshape(bf16[64,128,1536]{2,1,0:T(8,128)(2,1)} %gather_fusion.1) | data formatting | bytes 50331648 | tf_op jit(solution)/shard_map/vmap(jit(_take))/gather | solution.py:58
  500.9 41.2 %copy.77 = bf16[2,4096,12,128]{1,3,2,0:T(8,128)(2,1)} copy(bf16[2,4096,12,128]{3,2,1,0:T(8,128)(2,1)} %reshape.736) | data formatting | bytes 50331648 | tf_op jit(solution)/shard_map/vmap(jit(_take))/gather | solution.py:58
  626.0 60.1 %copy.80 = bf16[2,4096,2048]{1,0,2:T(2,128)(2,1)} copy(bf16[2,4096,2048]{1,2,0:T(8,128)(2,1)} %bitcast_select_fusion) | data formatting | bytes 67108864 | tf_op jit(solution)/shard_map/vmap(jit(_take))/select_n | solution.py:58
  693.8 30.0 %copy.110 = f32[512,8,16,128]{3,1,2,0:T(8,128)} copy(f32[512,8,16,128]{3,2,1,0:T(8,128)} %bitcast.157) | data formatting | bytes 67108864
  723.8 31.2 %copy.93 = f32[4096,2048]{0,1:T(8,128)} copy(f32[4096,2048]{1,0:T(8,128)} %bitcast.153) | data formatting | bytes 67108864 | tf_op jit(solution)/shard_map/reshape | solution.py:129
  755.0 662.6 %all-to-all-done.1 = bf16[2,4096,2048]{1,0,2:T(2,128)(2,1)} async-done(((bf16[2,4096,2048]{1,0,2:T(2,128)(2,1)}), bf16[2,4096,2048]{1,0,2:T(2,128)(2,1)}, u32[]{:S(2)}, u32[]{:S(2)}) %all-to-all-start.1) | async-done | bytes 33554464 | tf_op jit(solution)/shard_map/all_to_all | solution.py:97
  1417.6 29.6 %copy.81 = bf16[2,4096,2048]{1,2,0:T(8,128)(2,1)} copy(bf16[2,4096,2048]{1,0,2:T(2,128)(2,1)} %all-to-all-done.1) | data formatting | bytes 67108864 | tf_op jit(solution)/shard_map/all_to_all | solution.py:97
  1447.2 23.1 concatenate.54
  1470.3 23.0 gather_fusion.3
  1493.3 33.0 %convert_reduce_fusion = f32[16,4096,128]{1,2,0:T(8,128)} fusion(bf16[2,16,4096,128]{2,3,1,0:T(8,128)(2,1)} %bitcast.149, pred[2,16]{1,0:T(4,128)(4,1)S(1)} %copy-done.9), kind=kLoop, calls=%fused_computation.14 | loop fusion | flops 41943040 | bytes 67108896 | tf_op jit(solution)/shard_map/reduce_sum | solution.py:128
  1526.2 33.5 %bitcast_add_fusion = f32[4096,2048]{0,1:T(8,128)} fusion(f32[4096,2048]{0,1:T(8,128)} %copy.93, f32[16,4096,128]{1,2,0:T(8,128)} %convert_reduce_fusion), kind=kLoop, calls=%fused_computation.16 | loop fusion | flops 8388608 | bytes 100663296 | tf_op jit(solution)/shard_map/add | solution.py:129
  1564.4 153.2 %all-reduce.12.cloned.1.call-done = f32[4096,256]{0,1:T(8,128)} async-done(((f32[4096,256]{0,1:T(8,128)}), f32[4096,256]{0,1:T(8,128)}) %all-reduce.12.cloned.1.call-update) | async-done | bytes 4194320 | tf_op jit(solution)/shard_map/psum | solution.py:159
  1719.6 31.4 %all-reduce.14.cloned.1.call-done = f32[256,256]{0,1:T(8,128)} async-done(((f32[256,256]{0,1:T(8,128)}), f32[256,256]{0,1:T(8,128)}) %all-reduce.14.cloned.1.call-update) | async-done | bytes 262160 | tf_op jit(solution)/shard_map/psum | solution.py:171
  1863.3 51.5 %all-reduce.16.cloned.1.call-done = f32[2048,256]{0,1:T(8,128)} async-done(((f32[2048,256]{0,1:T(8,128)}), f32[2048,256]{0,1:T(8,128)}) %all-reduce.16.cloned.1.call-update) | async-done | bytes 2097168 | tf_op jit(solution)/shard_map/psum | solution.py:13
  1914.7 36.0 %convolution_subtract_fusion.1 = f32[4096,2048]{0,1:T(8,128)} fusion(f32[4096,2048]{0,1:T(8,128)} %bitcast_add_fusion, f32[4096,256]{0,1:T(8,128)} %fusion, f32[2048,256]{0,1:T(8,128)} %all-reduce.16.cloned.1.call-done), kind=kOutput, calls=%fused_computation.22 | convolution fusion | flops 25778192384 | bytes 73400320 | tf_op jit(solution)/shard_map/dot_general | solution.py:187
  1955.3 156.5 %all-reduce.18.cloned.1.call-done = f32[4096,256]{0,1:T(8,128)} async-done(((f32[4096,256]{0,1:T(8,128)}), f32[4096,256]{0,1:T(8,128)}) %all-reduce.18.cloned.1.call-update) | async-done | bytes 4194320 | tf_op jit(solution)/shard_map/psum | solution.py:159
  2113.8 31.2 %all-reduce.20.cloned.1.call-done = f32[256,256]{0,1:T(8,128)} async-done(((f32[256,256]{0,1:T(8,128)}), f32[256,256]{0,1:T(8,128)}) %all-reduce.20.cloned.1.call-update) | async-done | bytes 262160 | tf_op jit(solution)/shard_map/psum | solution.py:171
  2258.1 50.8 %all-reduce.22.cloned.1.call-done = f32[2048,256]{0,1:T(8,128)} async-done(((f32[2048,256]{0,1:T(8,128)}), f32[2048,256]{0,1:T(8,128)}) %all-reduce.22.cloned.1.call-update) | async-done | bytes 2097168 | tf_op jit(solution)/shard_map/psum | solution.py:13
  2308.9 36.1 %convolution_subtract_fusion = f32[4096,2048]{0,1:T(8,128)} fusion(f32[4096,2048]{0,1:T(8,128)} %convolution_subtract_fusion.1, f32[4096,256]{0,1:T(8,128)} %fusion.1, f32[2048,256]{0,1:T(8,128)} %all-reduce.22.cloned.1.call-done), kind=kOutput, calls=%fused_computation.21 | convolution fusion | flops 25778192384 | bytes 73400320 | tf_op jit(solution)/shard_map/dot_general | solution.py:187
  2381.8 42.8 %copy.89 = f32[32,128,16,128]{3,2,1,0:T(8,128)} copy(f32[32,128,16,128]{1,0,3,2:T(8,128)} %bitcast.152) | data formatting | bytes 67108864 | tf_op jit(solution)/shard_map/reshape | solution.py:208
  (189 shorter events, 486.0 us)
Async XLA Ops:
  205.0 7.7 copy-start.8
  205.0 213.8 %all-to-all-start = ((bf16[2,3072,1536]{2,0,1:T(2,128)(2,1)}), bf16[2,3072,1536]{2,0,1:T(2,128)(2,1)}, u32[]{:S(2)}, u32[]{:S(2)}) async-start(bf16[2,3072,1536]{2,0,1:T(2,128)(2,1)} %copy.74), calls=%async_computation | async-start | bytes 37748736 | tf_op jit(solution)/shard_map/all_to_all | solution.py:77
  235.7 195.0 %copy-start = (s32[2,17]{1,0:T(2,128)}, s32[2,17]{1,0:T(2,128)S(1)}, u32[]{:S(2)}) copy-start(s32[2,17]{1,0:T(2,128)S(1)} %scatter_fusion) | copy-start | bytes 412
  686.1 7.6 copy-start.1
  686.1 731.5 %all-to-all-start.1 = ((bf16[2,4096,2048]{1,0,2:T(2,128)(2,1)}), bf16[2,4096,2048]{1,0,2:T(2,128)(2,1)}, u32[]{:S(2)}, u32[]{:S(2)}) async-start(bf16[2,4096,2048]{1,0,2:T(2,128)(2,1)} %copy.80), calls=%async_computation.1 | async-start | bytes 67108864 | tf_op jit(solution)/shard_map/all_to_all | solution.py:97
  693.2 1024.4 %all-reduce.12.cloned.1.call-start = ((), (), s32[]{:S(2)}) async-start(), calls=%async_computation.2 | async-start | bytes 8388608 | tf_op jit(solution)/shard_map/psum | solution.py:159
  1470.3 23.0 copy-start.9
  1564.3 186.7 %all-reduce.14.cloned.1.call-start = ((), (), s32[]{:S(2)}) async-start(), calls=%async_computation.3 | async-start | bytes 524288 | tf_op jit(solution)/shard_map/psum | solution.py:171
  1719.3 195.4 %all-reduce.16.cloned.1.call-start = ((), (), s32[]{:S(2)}) async-start(), calls=%async_computation.4 | async-start | bytes 4194304 | tf_op jit(solution)/shard_map/psum | solution.py:13
  1835.0 3.7 copy-start.6
  1838.7 4.0 copy-start.5
  1863.2 248.6 %all-reduce.18.cloned.1.call-start = ((), (), s32[]{:S(2)}) async-start(), calls=%async_computation.5 | async-start | bytes 8388608 | tf_op jit(solution)/shard_map/psum | solution.py:159
  1955.2 189.7 %all-reduce.20.cloned.1.call-start = ((), (), s32[]{:S(2)}) async-start(), calls=%async_computation.6 | async-start | bytes 524288 | tf_op jit(solution)/shard_map/psum | solution.py:171
  2113.4 195.5 %all-reduce.22.cloned.1.call-start = ((), (), s32[]{:S(2)}) async-start(), calls=%async_computation.7 | async-start | bytes 4194304 | tf_op jit(solution)/shard_map/psum | solution.py:13
  2229.5 3.7 copy-start.7
  2233.1 4.0 copy-start.4
  2308.9 36.1 %copy-start.2 = (f32[4096,256]{0,1:T(8,128)S(1)}, f32[4096,256]{0,1:T(8,128)}, u32[]{:S(2)}) copy-start(f32[4096,256]{0,1:T(8,128)} %fusion) | copy-start | bytes 12582916
  2349.0 2.5 copy-start.3
Sparse Core Ops, SparseCore 0:
  1564.4 153.1 all-reduce.11
  1719.9 30.9 all-reduce.13
  1863.3 51.3 all-reduce.15
  1955.4 156.3 all-reduce.17
  2113.9 30.9 all-reduce.19
  2257.5 51.3 all-reduce.21
where the time goes:
time: 2440 us; the launch traced here: 2430 us
  waiting for transfers between devices  1320 us (54%)
  local copies, waits for them, and re-layouts  698 us (29%)
  other arithmetic  293 us (12%)
  matrix products  88.3 us (4%)
    all_to_all x1, waiting for transfers between devices, move_columns(): lax.all_to_all(outgoing, 'col', split_axis=2, concat_axis=2, tiled=True)  663 us
    psum x2, waiting for transfers between devices, on_device(): panel_rows = lax.psum(jnp.concatenate(pieces, axis=1), 'col')  310 us
    gather x11, local copies, waits for them, and re-layouts, pick_slots(): jnp.take(part_data, part_index, axis=axis_no)  189 us
    all_to_all x1, waiting for transfers between devices, move_rows(): lax.all_to_all(outgoing, 'row', split_axis=1, concat_axis=1, tiled=True)  183 us
    select_n x2, local copies, waits for them, and re-layouts, pick_slots(): jnp.take(part_data, part_index, axis=axis_no)  163 us
    psum x2, waiting for transfers between devices, spread_2(): return lax.psum(kept, axis)  102 us
    dot_general x2, matrix products, on_device(): jnp.dot(lower_part, col_part.T, precision=lax.Precision.HIGHEST, preferre...  72.1 us
    unnamed x31, local copies, waits for them, and re-layouts  71.9 us
  transfers between devices with their start and end apart: 8, of which 8 were waited for; matrix products, arithmetic and copies ran while one was open for 4% of the time, Pallas kernels for 0%

commit v1 on v0

v1 whole, which is shorter than its diff:
```python
import functools

import jax
import jax.numpy as jnp
from jax import lax
from jax.experimental import pallas as pl
from jax.experimental.pallas import tpu as pltpu
from jax.sharding import Mesh, PartitionSpec as P

PD = 512
TILE = 128
PT = PD // TILE
COL = ("half", "lane")
AXES = ("row",) + COL
VMEM_LIMIT = 48 * 1024 * 1024


class Plan:
    def __init__(self, rows, lanes, groups, homes):
        self.R, self.L, self.G = rows, lanes, groups
        self.cap_r = -(-groups // rows)
        self.cap_l = -(-groups // lanes)
        self.shift = 0
        self.home = self.shift + 2 * groups
        self.by_class = self.home + 2 * groups
        self.by_shift = self.by_class + 2 * rows * self.cap_r
        self.first = self.by_shift + 2 * lanes * self.cap_l
        self.homes = homes
        self.at_home = self.first + 2
        self.rank = self.at_home + 2 * homes
        self.rho = self.rank + 2 * groups
        self.kap = self.rho + 1

    def get_shift(self, tab, i, a):
        return tab[self.shift + i * self.G + a]

    def get_home(self, tab, i, a):
        return tab[self.home + i * self.G + a]

    def class_entry(self, tab, i, m, t):
        return tab[self.by_class + (i * self.R + m) * self.cap_r + t]

    def shift_entry(self, tab, i, s, t):
        return tab[self.by_shift + (i * self.L + s) * self.cap_l + t]

    def place(self, tab):
        kap = tab[self.kap]
        return tab[self.rho], kap // self.R, lax.rem(kap, self.R)


def make_table(plan, child_map):
    R, L, G = plan.R, plan.L, plan.G
    lead = child_map.reshape(2, G, L)[:, :, 0]
    shift, home = lead % L, lead // L
    ids = jnp.arange(G, dtype=jnp.int32)
    before = ids[None, :] < ids[:, None]

    def inverse(keys, count, capacity):
        rank = jnp.sum((keys[:, :, None] == keys[:, None, :]) & before[None], axis=2)
        hit = (keys[:, None, None, :] == jnp.arange(count)[None, :, None, None]) & (
            rank[:, None, None, :] == jnp.arange(capacity)[None, None, :, None]
        )
        return jnp.max(jnp.where(hit, ids[None, None, None, :], -1), axis=3)

    at_home = inverse(home, plan.homes, 1)
    same = (shift % R)[:, :, None] == (shift % R)[:, None, :]
    rank = jnp.sum(same & before[None], axis=2)
    parts = [shift, home, inverse(shift % R, R, plan.cap_r), inverse(shift, L, plan.cap_l), at_home[:, 0], at_home, rank]
    here = [lax.axis_index("row"), lax.axis_index(COL)]
    return jnp.concatenate(
        [p.reshape(-1).astype(jnp.int32) for p in parts] + [h.reshape(1).astype(jnp.int32) for h in here]
    )


def modr(value, n):
    return lax.rem(value + 2 * n, n)


def pack_near(plan, table, updates):
    R, L = plan.R, plan.L
    slots = updates.shape[2]

    def body(tab, x_ref, out):
        i = pl.program_id(0)
        kap = tab[plan.kap]
        for k in range(L):
            for t in range(plan.cap_l):
                b = plan.shift_entry(tab, i, lax.rem(kap + k, L), t)

                @pl.when(b >= 0)
                def _(k=k, t=t, b=b):
                    out[0, k // R, k % R, 0, 0, t] = x_ref[0, 0, b]

    def in_map(i, r, t, tab):
        rho, h, _ = plan.place(tab)
        return (i, 2 * jnp.maximum(plan.class_entry(tab, i, lax.rem(r + rho, R), t), 0) + h, 0, 0, 0)

    shape = (R, 2, R, 2, plan.cap_r, plan.cap_l, TILE, TILE)
    return pl.pallas_call(
        body,
        grid_spec=pltpu.PrefetchScalarGridSpec(
            num_scalar_prefetch=1,
            grid=(2, R, plan.cap_r),
            in_specs=[pl.BlockSpec((1, 1, slots, TILE, TILE), in_map)],
            out_specs=pl.BlockSpec(
                (1, 2, R, 1, 1, plan.cap_l, TILE, TILE), lambda i, r, t, tab: (r, 0, 0, i, t, 0, 0, 0)
            ),
        ),
        out_shape=jax.ShapeDtypeStruct(shape, jnp.bfloat16),
        compiler_params=pltpu.CompilerParams(vmem_limit_bytes=VMEM_LIMIT),
        name="pack_near",
    )(table, updates)


def pack_far(plan, table, updates):
    R, L = plan.R, plan.L
    slots = updates.shape[2]
    shape = jax.ShapeDtypeStruct((R, R, 2, 2, plan.cap_r, plan.cap_l, TILE, TILE), jnp.bfloat16)
    in_block = (1, 1, slots, TILE, TILE)

    def direct(tab, x_ref, out):
        i = pl.program_id(0)
        kap = tab[plan.kap]
        h = kap // R
        for k in range(R):
            for t in range(plan.cap_l):
                b = plan.shift_entry(tab, i, lax.rem(kap + h * R + k, L), t)

                @pl.when(b >= 0)
                def _(k=k, t=t, b=b):
                    out[0, k, 0, 0, 0, t] = x_ref[0, 0, b]

    def direct_map(i, r, t, tab):
        rho, h, _ = plan.place(tab)
        return (i, 2 * jnp.maximum(plan.class_entry(tab, i, lax.rem(r + rho, R), t), 0) + 1 - h, 0, 0, 0)

    def row_group(tab, i, k, t):
        return plan.shift_entry(tab, i, lax.rem(k + tab[plan.rho] + R, L), t)

    def turned(tab, x_ref, held, out):
        i = pl.program_id(0)
        _, _, kl = plan.place(tab)

        @pl.when(row_group(tab, i, pl.program_id(1), pl.program_id(2)) >= 0)
        def _():
            for r in range(R):
                for t in range(plan.cap_r):
                    a = plan.class_entry(tab, i, lax.rem(r + kl, R), t)

                    @pl.when(a >= 0)
                    def _(r=r, t=t, a=a):
                        out[r, 0, 0, 0, t, 0] = x_ref[0, 0, a].T

    def turned_map(i, k, t, tab):
        _, h, _ = plan.place(tab)
        return (i, 2 * jnp.maximum(row_group(tab, i, k, t), 0) + 1 - h, 0, 0, 0)

    partial = pl.pallas_call(
        direct,
        grid_spec=pltpu.PrefetchScalarGridSpec(
            num_scalar_prefetch=1,
            grid=(2, R, plan.cap_r),
            in_specs=[pl.BlockSpec(in_block, direct_map)],
            out_specs=pl.BlockSpec(
                (1, R, 1, 1, 1, plan.cap_l, TILE, TILE), lambda i, r, t, tab: (r, 0, i, 0, t, 0, 0, 0)
            ),
        ),
        out_shape=shape,
        compiler_params=pltpu.CompilerParams(vmem_limit_bytes=VMEM_LIMIT),
        name="pack_far_direct",
    )(table, updates)
    return pl.pallas_call(
        turned,
        grid_spec=pltpu.PrefetchScalarGridSpec(
            num_scalar_prefetch=1,
            grid=(2, R, plan.cap_l),
            in_specs=[pl.BlockSpec(in_block, turned_map), pl.BlockSpec(memory_space=pl.ANY)],
            out_specs=pl.BlockSpec(
                (R, 1, 1, 1, plan.cap_r, 1, TILE, TILE), lambda i, k, t, tab: (0, k, i, 1, 0, t, 0, 0)
            ),
        ),
        out_shape=shape,
        input_output_aliases={2: 0},
        compiler_params=pltpu.CompilerParams(vmem_limit_bytes=VMEM_LIMIT),
        name="pack_far_turned",
    )(table, updates, partial)


def pack_panel(plan, table, updates):
    R, L = plan.R, plan.L
    slots = updates.shape[2]

    def which(tab, i):
        rho, _, _ = plan.place(tab)
        a = tab[plan.first + i]
        s = plan.get_shift(tab, i, jnp.maximum(a, 0))
        low = modr(s - rho, L) < PT
        high = modr(s - rho - R, L) < PT
        return a, low, high

    def body(tab, x_ref, out):
        i = pl.program_id(0)
        a, low, high = which(tab, i)
        there = (a >= 0) & (low | high)

        for k in range(L):
            for t in range(plan.cap_l):
                b = plan.shift_entry(tab, i, lax.rem(tab[plan.kap] + k, L), t)

                @pl.when((b >= 0) & there)
                def _(k=k, t=t, b=b):
                    out[k, 0, t] = x_ref[0, 0, b]

    def in_map(i, tab):
        a, _, high = which(tab, i)
        return (i, 2 * jnp.maximum(a, 0) + high.astype(jnp.int32), 0, 0, 0)

    return pl.pallas_call(
        body,
        grid_spec=pltpu.PrefetchScalarGridSpec(
            num_scalar_prefetch=1,
            grid=(2,),
            in_specs=[pl.BlockSpec((1, 1, slots, TILE, TILE), in_map)],
            out_specs=pl.BlockSpec((L, 1, plan.cap_l, TILE, TILE), lambda i, tab: (0, i, 0, 0, 0)),
        ),
        out_shape=jax.ShapeDtypeStruct((L, 2, plan.cap_l, TILE, TILE), jnp.bfloat16),
        compiler_params=pltpu.CompilerParams(vmem_limit_bytes=VMEM_LIMIT),
        name="pack_panel",
    )(table, updates)


def assemble_panel(plan, table, front_rows, child_rows, slots):
    R, L = plan.R, plan.L

    def body(tab, f_ref, c0_ref, c1_ref, out):
        f = pl.program_id(0)
        for cs in range(slots):
            out[cs] = f_ref[0, pl.ds(cs, TILE, stride=slots), :]
        for i, c_ref in ((0, c0_ref), (1, c1_ref)):

            @pl.when(tab[plan.first + i] >= 0)
            def _(i=i, c_ref=c_ref):
                for k in range(L):
                    for t in range(plan.cap_l):
                        b = plan.shift_entry(tab, i, lax.rem(tab[plan.kap] + k, L), t)

                        @pl.when(b >= 0)
                        def _(k=k, t=t, b=b):
                            cs = plan.get_home(tab, i, b)
                            out[cs] = out[cs] + c_ref[0, k, 0, t].astype(jnp.float32)

    def child_map(i):
        def at(f, tab):
            s = plan.get_shift(tab, i, jnp.maximum(tab[plan.first + i], 0))
            return (lax.rem(modr(s - f, L), R), 0, i, 0, 0, 0)

        return at

    child_block = (1, L, 1, plan.cap_l, TILE, TILE)
    return pl.pallas_call(
        body,
        grid_spec=pltpu.PrefetchScalarGridSpec(
            num_scalar_prefetch=1,
            grid=(PT,),
            in_specs=[
                pl.BlockSpec((1, TILE * slots, TILE), lambda f, tab: (f, 0, 0)),
                pl.BlockSpec(child_block, child_map(0)),
                pl.BlockSpec(child_block, child_map(1)),
            ],
            out_specs=pl.BlockSpec((slots, TILE, TILE), lambda f, tab: (0, f, 0)),
        ),
        out_shape=jax.ShapeDtypeStruct((slots, PD, TILE), jnp.float32),
        compiler_params=pltpu.CompilerParams(vmem_limit_bytes=VMEM_LIMIT),
        name="assemble_panel",
    )(table, front_rows, child_rows, child_rows)


def split_bf16(x):
    high = x.astype(jnp.bfloat16)
    return high, (x - high.astype(jnp.float32)).astype(jnp.bfloat16)


def solve_blocks(inverse, blocks, wide):
    count = blocks.shape[0]
    pair = 2 if count % 2 == 0 else 1

    def body(inv, x, high, low, inv_high, inv_low):
        @pl.when(pl.program_id(0) == 0)
        def _():
            inv_high[...], inv_low[...] = split_bf16(inv[...])

        xs = [split_bf16(x[q]) for q in range(pair)]
        xh = jnp.concatenate([p[0] for p in xs], axis=1)
        xl = jnp.concatenate([p[1] for p in xs], axis=1)
        y = jnp.dot(inv_high[...], xh, preferred_element_type=jnp.float32)
        y += jnp.dot(inv_high[...], xl, preferred_element_type=jnp.float32)
        y += jnp.dot(inv_low[...], xh, preferred_element_type=jnp.float32)
        hi, lo = split_bf16(y)
        if wide:
            high[...], low[...] = hi, lo
        else:
            for q in range(pair):
                high[q], low[q] = hi[:, q * TILE : (q + 1) * TILE], lo[:, q * TILE : (q + 1) * TILE]

    if wide:
        shape, spec = (PD, count * TILE), pl.BlockSpec((PD, pair * TILE), lambda s: (0, s))
    else:
        shape, spec = (count, PD, TILE), pl.BlockSpec((pair, PD, TILE), lambda s: (s, 0, 0))
    whole = pl.BlockSpec((PD, PD), lambda s: (0, 0))
    return pl.pallas_call(
        body,
        grid=(count // pair,),
        in_specs=[whole, pl.BlockSpec((pair, PD, TILE), lambda s: (s, 0, 0))],
        out_specs=[spec, spec],
        out_shape=[jax.ShapeDtypeStruct(shape, jnp.bfloat16)] * 2,
        scratch_shapes=[pltpu.VMEM((PD, PD), jnp.bfloat16)] * 2,
        compiler_params=pltpu.CompilerParams(vmem_limit_bytes=VMEM_LIMIT),
        name="solve_blocks",
    )(inverse, blocks)


def slab_source(plan, tab, i, fr):
    a = tab[plan.at_home + i * plan.homes + fr // 2]
    lane = modr(plan.get_shift(tab, i, jnp.maximum(a, 0)) - tab[plan.rho] - plan.R * lax.rem(fr, 2), plan.L)
    return a, lax.rem(lane, plan.R), lane // plan.R


def add_blocks(plan, tab, i, fr, half, out, block, slots):
    R, L = plan.R, plan.L
    kap = tab[plan.kap]
    for k in range(R):
        for t in range(plan.cap_l):
            b = plan.shift_entry(tab, i, lax.rem(kap + half * R + k, L), t)
            cs = plan.get_home(tab, i, jnp.maximum(b, 0))

            @pl.when((b >= 0) & jnp.logical_not((cs == 0) & (kap < PT)))
            def _(k=k, t=t, cs=cs):
                at = pl.ds(cs, TILE, stride=slots)
                out[0, at, :] = out[0, at, :] + block(k, t).astype(jnp.float32)


def near_spec(plan, i):
    def at(fr, tab):
        a, low, half = slab_source(plan, tab, i, fr)
        rank = tab[plan.rank + i * plan.G + jnp.maximum(a, 0)]
        return (low, half, 0, i, rank, 0, 0, 0)

    return pl.BlockSpec((1, 1, plan.R, 1, 1, plan.cap_l, TILE, TILE), at)


def far_specs(plan, i):
    def direct(fr, tab):
        a, low, _ = slab_source(plan, tab, i, fr)
        return (low, 0, i, 0, tab[plan.rank + i * plan.G + jnp.maximum(a, 0)], 0, 0, 0)

    def turned(fr, tab):
        a, low, _ = slab_source(plan, tab, i, fr)
        return (0, low, i, 1, tab[plan.rank + i * plan.G + jnp.maximum(a, 0)], 0, 0, 0)

    return [
        pl.BlockSpec((1, plan.R, 1, 1, 1, plan.cap_l, TILE, TILE), direct),
        pl.BlockSpec((plan.R, 1, 1, 1, 1, plan.cap_l, TILE, TILE), turned),
    ]


def trailing(plan, table, front, factor, row_parts, col_parts, far, slots):
    R, L = plan.R, plan.L
    count = front.shape[0]
    per_lane = row_parts[0].shape[0] // 2

    def body(tab, f_ref, l_ref, rh, rl, ch, cl, direct0, turned0, direct1, turned1, out):
        fr = pl.program_id(0)
        rho, kap = tab[plan.rho], tab[plan.kap]
        head = (fr == 0) & (rho < PT)
        contract = (((0,), (0,)), ((), ()))
        step = 256 if slots % 2 == 0 else 128

        @pl.when(jnp.logical_not(head))
        def _():
            xh, xl = rh[0], rl[0]
            for w in range(slots * TILE // step):
                cols = pl.ds(w * step, step)
                y = lax.dot_general(xh, ch[:, cols], contract, preferred_element_type=jnp.float32)
                y += lax.dot_general(xh, cl[:, cols], contract, preferred_element_type=jnp.float32)
                y += lax.dot_general(xl, ch[:, cols], contract, preferred_element_type=jnp.float32)
                for q in range(step // TILE):
                    at = pl.ds(w * (step // TILE) + q, TILE, stride=slots)
                    out[0, at, :] = f_ref[0, at, :] - y[:, q * TILE : (q + 1) * TILE]

        h = kap // R
        for i, direct, turned in ((0, direct0, turned0), (1, direct1, turned1)):
            a, _, half = slab_source(plan, tab, i, fr)

            @pl.when((a >= 0) & jnp.logical_not(head) & (half != h))
            def _(i=i, direct=direct):
                add_blocks(plan, tab, i, fr, h, out, lambda k, t: direct[0, k, 0, 0, 0, t], slots)

            @pl.when((a >= 0) & jnp.logical_not(head) & (half == h))
            def _(i=i, turned=turned):
                add_blocks(plan, tab, i, fr, 1 - h, out, lambda k, t: turned[k, 0, 0, 0, 0, t], slots)

        @pl.when(head)
        def _():
            out[...] = jnp.zeros_like(out)

        @pl.when((kap < PT) & head)
        def _():
            out[0, pl.ds(0, TILE, stride=slots), :] = l_ref[...]

        @pl.when((kap < PT) & jnp.logical_not(head))
        def _():
            rows = pl.ds(pl.multiple_of(kap * TILE, TILE), TILE)
            x = rh[0, rows, :].astype(jnp.float32) + rl[0, rows, :].astype(jnp.float32)
            out[0, pl.ds(0, TILE, stride=slots), :] = x.T

    slab = pl.BlockSpec((1, TILE * slots, TILE), lambda fr, tab: (fr, 0, 0))
    row_spec = pl.BlockSpec((1, PD, TILE), lambda fr, tab: (lax.rem(fr, 2) * per_lane + fr // 2, 0, 0))
    col_spec = pl.BlockSpec((PD, slots * TILE), lambda fr, tab: (0, 0))
    factor_spec = pl.BlockSpec(
        (TILE, TILE), lambda fr, tab: (jnp.minimum(tab[plan.rho], PT - 1), jnp.minimum(tab[plan.kap], PT - 1))
    )
    flops = 6 * count * TILE * PD * slots * TILE
    return pl.pallas_call(
        body,
        grid_spec=pltpu.PrefetchScalarGridSpec(
            num_scalar_prefetch=1,
            grid=(count,),
            in_specs=[slab, factor_spec, row_spec, row_spec, col_spec, col_spec] + far_specs(plan, 0) + far_specs(plan, 1),
            out_specs=slab,
        ),
        out_shape=jax.ShapeDtypeStruct(front.shape, jnp.float32),
        compiler_params=pltpu.CompilerParams(vmem_limit_bytes=VMEM_LIMIT),
        cost_estimate=pl.CostEstimate(flops=flops, bytes_accessed=2 * front.size * 4, transcendentals=0),
        name="trailing",
    )(table, front, factor, *row_parts, *col_parts, far, far, far, far)


def add_near(plan, table, total, near, slots):
    def body(tab, t_ref, near0, near1, out):
        fr = pl.program_id(0)
        out[...] = t_ref[...]
        live = jnp.logical_not((fr == 0) & (tab[plan.rho] < PT))
        for i, near_ref in ((0, near0), (1, near1)):
            a, _, half = slab_source(plan, tab, i, fr)

            @pl.when(live & (a >= 0))
            def _(i=i, half=half, near_ref=near_ref):
                add_blocks(plan, tab, i, fr, half, out, lambda k, t: near_ref[0, 0, k, 0, 0, t], slots)

    slab = pl.BlockSpec((1, TILE * slots, TILE), lambda fr, tab: (fr, 0, 0))
    return pl.pallas_call(
        body,
        grid_spec=pltpu.PrefetchScalarGridSpec(
            num_scalar_prefetch=1,
            grid=(total.shape[0],),
            in_specs=[slab, near_spec(plan, 0), near_spec(plan, 1)],
            out_specs=slab,
        ),
        out_shape=jax.ShapeDtypeStruct(total.shape, jnp.float32),
        input_output_aliases={1: 0},
        compiler_params=pltpu.CompilerParams(vmem_limit_bytes=VMEM_LIMIT),
        name="add_near",
    )(table, total, near, near)


def permute(x, plan, target):
    R, L = plan.R, plan.L
    pairs = []
    for rho in range(R):
        for h in range(2):
            for kl in range(R):
                r2, h2, k2 = target(rho, h, kl)
                pairs.append((rho * L + h * R + kl, (r2 % R) * L + h2 * R + k2 % R))
    return lax.ppermute(x, AXES, pairs)


def panel_factor(diagonal):
    factor = jnp.linalg.cholesky(diagonal)
    inverse = lax.linalg.triangular_solve(
        factor, jnp.eye(PD, dtype=jnp.float32), left_side=True, lower=True
    )
    return factor, inverse


def scaled_half(block, largest):
    exponent = jnp.clip(jnp.ceil(jnp.log2(jnp.maximum(largest, 1e-30))), -100.0, 100.0)
    scaled = (block * jnp.exp2(-exponent)).astype(jnp.float16)
    return jnp.concatenate([scaled, jnp.full((16, TILE), exponent, jnp.float16)], axis=0)


def from_half(parts):
    exponent = parts[:, -1:, :1].astype(jnp.float32)
    return parts[:, :-16].astype(jnp.float32) * jnp.exp2(exponent)


def on_device(front_blocks, child_updates, child_map):
    R, L = lax.axis_size("row"), lax.axis_size(COL)
    front_rows, tile, slots, _ = front_blocks.shape
    plan = Plan(R, L, child_map.shape[1] // L, slots)
    table = make_table(plan, child_map)
    front = front_blocks.reshape(front_rows, tile * slots, tile)
    updates = jnp.transpose(child_updates, (0, 1, 3, 2, 4))

    table, first = lax.optimization_barrier((table, front[0]))
    front_head = lax.all_gather(first, "row")
    head = pack_panel(plan, table, updates)
    moved = lax.all_to_all(head, COL, 0, 0, tiled=True)

    def exchange(blocks, axes, count, after):
        flat, _ = lax.optimization_barrier((blocks.reshape((count, -1, TILE, TILE)), after))
        return lax.all_to_all(flat, axes, 0, 0, tiled=True).reshape(blocks.shape)

    far = pack_far(plan, table, updates)
    far_in = exchange(far, ("row", "lane"), R * R, (moved, front_head))

    child_head = lax.all_gather(moved, "row")
    near = pack_near(plan, table, updates)
    child_head, near = lax.optimization_barrier((child_head, near))
    panel = assemble_panel(plan, table, front_head, child_head, slots)
    diag_tiles = lax.all_gather(panel[0], COL)
    diagonal = jnp.concatenate([diag_tiles[k] for k in range(PT)], axis=1)
    count = slots // R
    piece = lax.dynamic_slice_in_dim(panel, lax.axis_index("row") * count, count, axis=0)
    piece = scaled_half(piece.reshape(count * PD, TILE), jnp.max(jnp.abs(panel)))
    piece, far_in = lax.optimization_barrier((piece, far_in))
    piece = permute(piece, plan, lambda rho, h, kl: (kl, h, rho))
    row_half = lax.all_gather(piece, COL)
    near_in = exchange(near, AXES, R * L, (row_half, diagonal))
    row_panel = from_half(row_half).reshape(L * count, PD, TILE)

    factor, inverse = panel_factor(diagonal)
    col_parts = solve_blocks(inverse, panel, True)
    row_parts = solve_blocks(inverse, row_panel, False)
    total = trailing(plan, table, front, factor, row_parts, col_parts, far_in, slots)
    near_in, total = lax.optimization_barrier((near_in, total))
    total = add_near(plan, table, total, near_in, slots)
    return total.reshape(front_blocks.shape)


def solution(mesh):
    rows, lanes = mesh.devices.shape
    split = Mesh(mesh.devices.reshape(rows, 2, lanes // 2), AXES)
    placed = (P(None, "row", None, COL), P(None, None, "row", None, COL), P())
    return jax.shard_map(
        on_device,
        mesh=split,
        in_specs=placed,
        out_specs=P(None, "row", None, COL),
        check_vma=False,
    )
```

time: 2440 us -> 695 us (0.28)
  waiting for transfers between devices: 1320 us -> 187 us
  local copies, waits for them, and re-layouts: 698 us -> 28 us
  Pallas kernels: 0 us -> 206 us
  other arithmetic: 293 us -> 135 us
  blocking collectives: 0 us -> 83.5 us
  matrix products: 88.3 us -> 11.9 us
    all_to_all x2 -> x3, waiting for transfers between devices: 845 us -> 55.4 us  [the longest x2 55.4 us: exchange(): return lax.all_to_all(flat, axes, 0, 0, tiled=True).reshape(blocks.shape)]
    psum x6 -> x0, waiting for transfers between devices: 475 us -> none  [the longest x2 310 us: on_device(): panel_rows = lax.psum(jnp.concatenate(pieces, axis=1), 'col')]
    gather x15 -> x0, local copies, waits for them, and re-layouts: 233 us -> none  [the longest x11 189 us: pick_slots(): jnp.take(part_data, part_index, axis=axis_no)]
    pallas_call x0 -> x9, Pallas kernels: none -> 206 us  [the longest x1 79.3 us: trailing(): pl.pallas_call(body, grid_spec=pltpu.PrefetchScalarGridSpec(num_scalar_pr...]
    select_n x6 -> x3, local copies, waits for them, and re-layouts: 164 us -> 0.27 us  [the longest x2 0.18 us: make_table(): shift, home = (lead % L, lead // L)]
    all_gather x0 -> x3, waiting for transfers between devices: none -> 131 us  [the longest x1 90.4 us: on_device(): child_head = lax.all_gather(moved, 'row')]
    reshape x9 -> x5, local copies, waits for them, and re-layouts: 88.7 us -> 1.1 us  [the longest x1 0.76 us: make_table(): lead = child_map.reshape(2, G, L)[:, :, 0]]
    all_gather x0 -> x1, blocking collectives: none -> 83.5 us  [on_device(): row_half = lax.all_gather(piece, COL)]
  transfers between devices with their start and end apart: 8 -> 7, of which waited for: 8 -> 4; matrix products, arithmetic and copies ran while one was open for 4% -> 24% of each run, Pallas kernels for 0% -> 24%
where the time goes in v1:
time: 695 us; the launch traced here: 688 us
  Pallas kernels  206 us (30%)
  waiting for transfers between devices  187 us (27%)
  other arithmetic  135 us (19%)
  blocking collectives  83.5 us (12%)
  local copies, waits for them, and re-layouts  28 us (4%)
  starting transfers between devices  18.6 us (3%)
  between operations  17.1 us (2%)
  matrix products  11.9 us (2%)
    all_gather x1, waiting for transfers between devices, on_device(): child_head = lax.all_gather(moved, 'row')  90.4 us
    all_gather x1, blocking collectives, on_device(): row_half = lax.all_gather(piece, COL)  83.5 us
    pallas_call x1, Pallas kernels, trailing(): pl.pallas_call(body, grid_spec=pltpu.PrefetchScalarGridSpec(num_scalar_pr...  79.3 us
    another operation x14, other arithmetic, panel_factor(): factor = jnp.linalg.cholesky(diagonal)  78.5 us
    all_to_all x2, waiting for transfers between devices, exchange(): return lax.all_to_all(flat, axes, 0, 0, tiled=True).reshape(blocks.shape)  55.4 us
    another operation x4, other arithmetic, panel_factor(): lax.linalg.triangular_solve(factor, jnp.eye(PD, dtype=jnp.float32), left_...  41.4 us
    all_gather x1, waiting for transfers between devices, on_device(): diag_tiles = lax.all_gather(panel[0], COL)  40.8 us
    pallas_call x1, Pallas kernels, add_near(): pl.pallas_call(body, grid_spec=pltpu.PrefetchScalarGridSpec(num_scalar_pr...  40.7 us
  transfers between devices with their start and end apart: 7, of which 4 were waited for; matrix products, arithmetic and copies ran while one was open for 24% of the time, Pallas kernels for 24%

profile of v1, /device:TPU:0, one launch (start us, length us, event | category | flops | bytes accessed | tf_op | source)
XLA Modules:
  0.0 687.8 jit_solution(6861854902000919752)
XLA Ops:
  16.1 7.3 %all-to-all-start = ((bf16[8,2,2,128,128]{4,3,2,1,0:T(8,128)(2,1)}), bf16[8,2,2,128,128]{4,3,2,1,0:T(8,128)(2,1)S(1)}, u32[]{:S(2)}, u32[]{:S(2)}) async-start(bf16[8,2,2,128,128]{4,3,2,1,0:T(8,128)(2,1)} %pack_panel.1), calls=%async_computation | async-start | bytes 2097152 | tf_op jit(solution)/shard_map/all_to_all | solution.py:507
  23.4 16.1 %pack_far_direct.1.held = bf16[4,4,2,2,3,2,128,128]{7,6,5,4,3,2,1,0:T(8,128)(2,1)} custom-call(s32[164]{0:T(256)S(1)} %concatenate.17.tab, bf16[2,24,12,128,128]{4,3,2,1,0:T(8,128)(2,1)} %bitcast.100), custom_call_target="tpu_custom_call" | custom-call | tf_op jit(solution)/shard_map/pack_far_direct/pallas_call | solution.py:158
  39.5 18.4 %pack_far_turned.1 = bf16[4,4,2,2,3,2,128,128]{7,6,5,4,3,2,1,0:T(8,128)(2,1)} custom-call(s32[164]{0:T(256)S(1)} %concatenate.17.tab, bf16[2,24,12,128,128]{4,3,2,1,0:T(8,128)(2,1)} %bitcast.101, bf16[4,4,2,2,3,2,128,128]{7,6,5,4,3,2,1,0:T(8,128)(2,1)} %pack_far_direct.1.held), custom_call_target="tpu_custom_call", output_to_operand_aliasing={{}: (2, {})} | custom-call | tf_op jit(solution)/shard_map/pack_far_turned/pallas_call | solution.py:172
  65.2 18.4 %pack_near.1 = bf16[4,2,4,2,3,2,128,128]{7,6,5,4,3,2,1,0:T(8,128)(2,1)} custom-call(s32[164]{0:T(256)S(1)} %concatenate.17.tab, bf16[2,24,12,128,128]{4,3,2,1,0:T(8,128)(2,1)} %bitcast.102), custom_call_target="tpu_custom_call" | custom-call | tf_op jit(solution)/shard_map/pack_near/pallas_call | solution.py:99
  83.6 90.4 %all-gather.10.cloned.1.call-done = bf16[32,2,2,128,128]{4,3,2,1,0:T(8,128)(2,1)} async-done(((bf16[8,2,2,128,128]{4,3,2,1,0:T(8,128)(2,1)}), bf16[32,2,2,128,128]{4,3,2,1,0:T(8,128)(2,1)}) %all-gather.10.cloned.1.call-update) | async-done | bytes 4194320 | tf_op jit(solution)/shard_map/all_gather | solution.py:516
  174.0 7.1 %assemble_panel.1.x = f32[16,512,128]{2,1,0:T(8,128)S(1)} custom-call(s32[164]{0:T(256)S(1)} %concatenate.17.tab, f32[4,2048,128]{2,1,0:T(8,128)} %bitcast.112, bf16[4,8,2,2,128,128]{5,4,3,2,1,0:T(8,128)(2,1)} %bitcast.109, bf16[4,8,2,2,128,128]{5,4,3,2,1,0:T(8,128)(2,1)} %bitcast.110), custom_call_target="tpu_custom_call" | custom-call | tf_op jit(solution)/shard_map/assemble_panel/pallas_call | solution.py:260
  189.8 36.1 %all-to-all-done.1 = bf16[16,24,128,128]{3,2,1,0:T(8,128)(2,1)} async-done(((bf16[16,24,128,128]{3,2,1,0:T(8,128)(2,1)}), bf16[16,24,128,128]{3,2,1,0:T(8,128)(2,1)}, u32[]{:S(2)}, u32[]{:S(2)}) %all-to-all-start.1) | async-done | bytes 12582944 | tf_op jit(solution)/shard_map/all_to_all | solution.py:511
  227.6 40.8 %all-gather.8.cloned.1.call-done = f32[8,512,128]{2,1,0:T(8,128)} async-done(((f32[1,512,128]{2,1,0:T(8,128)}), f32[8,512,128]{2,1,0:T(8,128)}) %all-gather.8.cloned.1.call-update) | async-done | bytes 2097168 | tf_op jit(solution)/shard_map/all_gather | solution.py:520
  270.3 83.5 %all-gather.13 = f16[16512,128]{1,0:T(8,128)(2,1)} all-gather(f16[2064,128]{1,0:T(8,128)(2,1)S(1)} %collective-permute-done), channel_id=4, replica_groups=mesh['row'=4,'half'=2,'lane'=4] {'half','lane'}, dimensions={0}, use_global_device_ids=true | all-gather | bytes 4755456 | tf_op jit(solution)/shard_map/all_gather | solution.py:527
  360.5 11.7 %cholesky.104 = f32[128,128]{1,0:T(8,128)S(1)} custom-call(f32[128,128]{1,0:T(8,128)S(1)} %cholesky.266), custom_call_target="Cholesky" | custom-call | tf_op jit(solution)/shard_map/jit(cholesky)/cholesky | solution.py:478
  372.2 9.8 %custom-call.30 = f32[1,128,128]{1,2,0:T(8,128)S(1)} custom-call(f32[1,128,128]{2,1,0:T(8,128)S(1)} %get-tuple-element.71), custom_call_target="InvertDiagBlocksLowerTriangular" | custom-call | tf_op jit(solution)/shard_map/jit(cholesky)/cholesky | solution.py:478
  384.7 11.7 %cholesky.217 = f32[128,128]{1,0:T(8,128)S(1)} custom-call(f32[128,128]{1,0:T(8,128)S(1)} %cholesky.270), custom_call_target="Cholesky" | custom-call | tf_op jit(solution)/shard_map/jit(cholesky)/cholesky | solution.py:478
  396.5 10.0 %custom-call.31 = f32[1,128,128]{1,2,0:T(8,128)S(1)} custom-call(f32[1,128,128]{2,1,0:T(8,128)S(1)} %get-tuple-element.68), custom_call_target="InvertDiagBlocksLowerTriangular" | custom-call | tf_op jit(solution)/shard_map/jit(cholesky)/cholesky | solution.py:478
  408.0 11.7 %cholesky.238 = f32[128,128]{1,0:T(8,128)S(1)} custom-call(f32[128,128]{1,0:T(8,128)S(1)} %cholesky.275), custom_call_target="Cholesky" | custom-call | tf_op jit(solution)/shard_map/jit(cholesky)/cholesky | solution.py:478
  419.8 9.8 %custom-call.32 = f32[1,128,128]{1,2,0:T(8,128)S(1)} custom-call(f32[1,128,128]{2,1,0:T(8,128)S(1)} %get-tuple-element.65), custom_call_target="InvertDiagBlocksLowerTriangular" | custom-call | tf_op jit(solution)/shard_map/jit(cholesky)/cholesky | solution.py:478
  431.0 11.7 %cholesky.255 = f32[128,128]{1,0:T(8,128)S(1)} custom-call(f32[128,128]{1,0:T(8,128)S(1)} %convolution_subtract_fusion.5), custom_call_target="Cholesky" | custom-call | tf_op jit(solution)/shard_map/jit(cholesky)/cholesky | solution.py:478
  448.5 14.1 %while.1 = (s32[]{:T(128)}, f32[512,512]{1,0:T(8,128)}, s32[4,2]{0,1:T(2,128)S(1)}, f32[4,128,128]{2,1,0:T(8,128)}, s32[]{:T(128)}) while((s32[]{:T(128)}, f32[512,512]{1,0:T(8,128)}, s32[4,2]{0,1:T(2,128)S(1)}, f32[4,128,128]{2,1,0:T(8,128)}, s32[]{:T(128)}) %tuple.52), condition=%wide.while_cond, body=%wide.while_body.sunk | while | flops 2 | bytes 132205 | solution.py:479
  462.6 40.1 %custom-call.33 = f32[4,128,128]{1,2,0:T(8,128)S(1)} custom-call(f32[4,128,128]{2,1,0:T(8,128)} %get-tuple-element.40), custom_call_target="InvertDiagBlocksLowerTriangular" | custom-call | tf_op jit(solution)/shard_map/triangular_solve | solution.py:479
  509.3 7.7 %solve_blocks.3 = (bf16[512,2048]{1,0:T(8,128)(2,1)S(1)}, bf16[512,2048]{1,0:T(8,128)(2,1)S(1)}) custom-call(f32[512,512]{1,0:T(8,128)S(1)} %pad_maximum_fusion.1.inv, f32[16,512,128]{2,1,0:T(8,128)} %copy-done), custom_call_target="tpu_custom_call" | custom-call | tf_op jit(solution)/shard_map/solve_blocks/pallas_call | solution.py:310
  517.9 6.3 convert_multiply_fusion
  524.1 15.5 %solve_blocks.2 = (bf16[32,512,128]{2,1,0:T(8,128)(2,1)S(1)}, bf16[32,512,128]{2,1,0:T(8,128)(2,1)}) custom-call(f32[512,512]{1,0:T(8,128)S(1)} %pad_maximum_fusion.1.inv, f32[32,512,128]{2,1,0:T(8,128)} %bitcast.106), custom_call_target="tpu_custom_call" | custom-call | tf_op jit(solution)/shard_map/solve_blocks/pallas_call | solution.py:310
  541.5 79.3 %trailing.1.t_ref = f32[32,2048,128]{2,1,0:T(8,128)} custom-call(s32[164]{0:T(256)S(1)} %concatenate.17.tab, f32[32,2048,128]{2,1,0:T(8,128)} %bitcast.105, f32[512,512]{1,0:T(8,128)S(1)} %get-tuple-element.53.l_ref, bf16[32,512,128]{2,1,0:T(8,128)(2,1)} %copy-done.1, bf16[32,512,128]{2,1,0:T(8,128)(2,1)} %get-tuple-element.27.rl, ...), custom_call_target="tpu_custom_call" | custom-call | flops 25769803776 | bytes 67108864 | tf_op jit(solution)/shard_map/trailing/pallas_call | solution.py:423
  620.8 19.3 %all-to-all-done.2 = bf16[32,12,128,128]{3,2,1,0:T(8,128)(2,1)} async-done(((bf16[32,12,128,128]{3,2,1,0:T(8,128)(2,1)}), bf16[32,12,128,128]{3,2,1,0:T(8,128)(2,1)}, u32[]{:S(2)}, u32[]{:S(2)}) %all-to-all-start.2) | async-done | bytes 12582944 | tf_op jit(solution)/shard_map/all_to_all | solution.py:511
  640.1 40.7 %add_near.1 = f32[32,2048,128]{2,1,0:T(8,128)} custom-call(s32[164]{0:T(256)S(1)} %concatenate.17.tab, f32[32,2048,128]{2,1,0:T(8,128)} %trailing.1.t_ref, bf16[4,2,4,2,3,2,128,128]{7,6,5,4,3,2,1,0:T(8,128)(2,1)} %bitcast.19.near0.near1, bf16[4,2,4,2,3,2,128,128]{7,6,5,4,3,2,1,0:T(8,128)(2,1)} %bitcast.19.near0.near1), custom_call_target="tpu_custom_call", output_to_operand_aliasing={{}: (1, {})} | custom-call | tf_op jit(solution)/shard_map/add_near/pallas_call | solution.py:451
  (116 shorter events, 67.3 us)
Async XLA Ops:
  6.5 51.3 %all-gather.12.cloned.1.call-start = ((), (), s32[]{:S(2)}) async-start(), calls=%async_computation.5 | async-start | bytes 5242880 | tf_op jit(solution)/shard_map/all_gather | solution.py:505
  16.1 41.8 %all-to-all-start = ((bf16[8,2,2,128,128]{4,3,2,1,0:T(8,128)(2,1)}), bf16[8,2,2,128,128]{4,3,2,1,0:T(8,128)(2,1)S(1)}, u32[]{:S(2)}, u32[]{:S(2)}) async-start(bf16[8,2,2,128,128]{4,3,2,1,0:T(8,128)(2,1)} %pack_panel.1), calls=%async_computation | async-start | bytes 2097152 | tf_op jit(solution)/shard_map/all_to_all | solution.py:507
  57.9 1.0 copy-start.2
  58.8 167.0 %all-to-all-start.1 = ((bf16[16,24,128,128]{3,2,1,0:T(8,128)(2,1)}), bf16[16,24,128,128]{3,2,1,0:T(8,128)(2,1)}, u32[]{:S(2)}, u32[]{:S(2)}) async-start(bf16[16,24,128,128]{3,2,1,0:T(8,128)(2,1)} %bitcast.103), calls=%async_computation.1 | async-start | bytes 25165824 | tf_op jit(solution)/shard_map/all_to_all | solution.py:511
  64.4 109.6 %all-gather.10.cloned.1.call-start = ((), (), s32[]{:S(2)}) async-start(), calls=%async_computation.4 | async-start | bytes 5242880 | tf_op jit(solution)/shard_map/all_gather | solution.py:516
  65.2 203.2 %all-gather.8.cloned.1.call-start = ((), (), s32[]{:S(2)}) async-start(), calls=%async_computation.3 | async-start | bytes 2359296 | tf_op jit(solution)/shard_map/all_gather | solution.py:520
  181.1 1.9 copy-start
  225.9 44.5 %collective-permute-start = (f16[2064,128]{1,0:T(8,128)(2,1)}, f16[2064,128]{1,0:T(8,128)(2,1)S(1)}, u32[]{:S(2)}, u32[]{:S(2)}) collective-permute-start(f16[2064,128]{1,0:T(8,128)(2,1)} %concatenate.18), channel_id=1, source_target_pairs={{0,0},{1,8},{2,16},{3,24},{4,4},{5,12},{6,20},{7,28},{8,1},{9,9},{... | collective-permute-start | bytes 1585160 | tf_op jit(solution)/shard_map/ppermute | solution.py:474
  269.9 83.9 %copy-start.4 = (f32[1,512,128]{1,2,0:T(8,128)}, f32[1,512,128]{1,2,0:T(8,128)S(1)}, u32[]{:S(2)}) copy-start(f32[1,512,128]{1,2,0:T(8,128)S(1)} %copy.47) | copy-start | bytes 786436
  270.1 83.7 %copy-start.5 = (f32[1,512,128]{1,2,0:T(8,128)}, f32[1,512,128]{1,2,0:T(8,128)S(1)}, u32[]{:S(2)}) copy-start(f32[1,512,128]{1,2,0:T(8,128)S(1)} %copy.46) | copy-start | bytes 786436
  270.2 83.6 %copy-start.6 = (f32[1,512,128]{1,2,0:T(8,128)}, f32[1,512,128]{1,2,0:T(8,128)S(1)}, u32[]{:S(2)}) copy-start(f32[1,512,128]{1,2,0:T(8,128)S(1)} %copy.48) | copy-start | bytes 786436
  353.8 286.3 %all-to-all-start.2 = ((bf16[32,12,128,128]{3,2,1,0:T(8,128)(2,1)}), bf16[32,12,128,128]{3,2,1,0:T(8,128)(2,1)}, u32[]{:S(2)}, u32[]{:S(2)}) async-start(bf16[32,12,128,128]{3,2,1,0:T(8,128)(2,1)} %bitcast.104), calls=%async_computation.2 | async-start | bytes 25165824 | tf_op jit(solution)/shard_map/all_to_all | solution.py:511
  360.5 11.8 %copy-start.3 = (f32[512,512]{1,0:T(8,128)}, f32[512,512]{1,0:T(8,128)S(1)}, u32[]{:S(2)}) copy-start(f32[512,512]{1,0:T(8,128)S(1)} %fusion) | copy-start | bytes 3145732
  539.6 1.9 copy-start.1
Sparse Core Ops, SparseCore 0:
  13.3 37.1 all-gather.11
  66.8 107.1 all-gather.9
  183.9 84.4 all-gather.7

commit v2 on v1

--- a/solution.py
+++ b/solution.py
@@ -13,6 +13,7 @@
 COL = ("half", "lane")
 AXES = ("row",) + COL
 VMEM_LIMIT = 48 * 1024 * 1024
+STREAMS = 4
 
 
 class Plan:
@@ -283,13 +284,14 @@
 def solve_blocks(inverse, blocks, wide):
     count = blocks.shape[0]
     pair = 2 if count % 2 == 0 else 1
+    height = blocks.shape[1]
 
     def body(inv, x, high, low, inv_high, inv_low):
         @pl.when(pl.program_id(0) == 0)
         def _():
             inv_high[...], inv_low[...] = split_bf16(inv[...])
 
-        xs = [split_bf16(x[q]) for q in range(pair)]
+        xs = [split_bf16(x[q] if height == PD else decode(x[q])) for q in range(pair)]
         xh = jnp.concatenate([p[0] for p in xs], axis=1)
         xl = jnp.concatenate([p[1] for p in xs], axis=1)
         y = jnp.dot(inv_high[...], xh, preferred_element_type=jnp.float32)
@@ -310,7 +312,7 @@
     return pl.pallas_call(
         body,
         grid=(count // pair,),
-        in_specs=[whole, pl.BlockSpec((pair, PD, TILE), lambda s: (s, 0, 0))],
+        in_specs=[whole, pl.BlockSpec((pair, height, TILE), lambda s: (s, 0, 0))],
         out_specs=[spec, spec],
         out_shape=[jax.ShapeDtypeStruct(shape, jnp.bfloat16)] * 2,
         scratch_shapes=[pltpu.VMEM((PD, PD), jnp.bfloat16)] * 2,
@@ -336,16 +338,7 @@
             @pl.when((b >= 0) & jnp.logical_not((cs == 0) & (kap < PT)))
             def _(k=k, t=t, cs=cs):
                 at = pl.ds(cs, TILE, stride=slots)
-                out[0, at, :] = out[0, at, :] + block(k, t).astype(jnp.float32)
-
-
-def near_spec(plan, i):
-    def at(fr, tab):
-        a, low, half = slab_source(plan, tab, i, fr)
-        rank = tab[plan.rank + i * plan.G + jnp.maximum(a, 0)]
-        return (low, half, 0, i, rank, 0, 0, 0)
-
-    return pl.BlockSpec((1, 1, plan.R, 1, 1, plan.cap_l, TILE, TILE), at)
+                out[at, :] = out[at, :] + block(k, t).astype(jnp.float32)
 
 
 def far_specs(plan, i):
@@ -393,11 +386,11 @@
 
             @pl.when((a >= 0) & jnp.logical_not(head) & (half != h))
             def _(i=i, direct=direct):
-                add_blocks(plan, tab, i, fr, h, out, lambda k, t: direct[0, k, 0, 0, 0, t], slots)
+                add_blocks(plan, tab, i, fr, h, out.at[0], lambda k, t: direct[0, k, 0, 0, 0, t], slots)
 
             @pl.when((a >= 0) & jnp.logical_not(head) & (half == h))
             def _(i=i, turned=turned):
-                add_blocks(plan, tab, i, fr, 1 - h, out, lambda k, t: turned[k, 0, 0, 0, 0, t], slots)
+                add_blocks(plan, tab, i, fr, 1 - h, out.at[0], lambda k, t: turned[k, 0, 0, 0, 0, t], slots)
 
         @pl.when(head)
         def _():
@@ -436,31 +429,99 @@
 
 
 def add_near(plan, table, total, near, slots):
-    def body(tab, t_ref, near0, near1, out):
-        fr = pl.program_id(0)
-        out[...] = t_ref[...]
-        live = jnp.logical_not((fr == 0) & (tab[plan.rho] < PT))
-        for i, near_ref in ((0, near0), (1, near1)):
-            a, _, half = slab_source(plan, tab, i, fr)
-
-            @pl.when(live & (a >= 0))
-            def _(i=i, half=half, near_ref=near_ref):
-                add_blocks(plan, tab, i, fr, half, out, lambda k, t: near_ref[0, 0, k, 0, 0, t], slots)
-
-    slab = pl.BlockSpec((1, TILE * slots, TILE), lambda fr, tab: (fr, 0, 0))
+    R = plan.R
+    count, rows = total.shape[0], TILE * slots
+    part = rows // STREAMS
+
+    def body(tab, t_hbm, near_hbm, out_hbm, slab, blocks, load_sem, near_sem, store_sem):
+        def loads(s, slot):
+            copies = []
+            for c in range(STREAMS):
+                at = pl.ds(c * part, part)
+                copies.append(
+                    pltpu.make_async_copy(t_hbm.at[s, at], slab.at[slot, at], load_sem.at[slot, c])
+                )
+            for i in range(2):
+                a, low, half = slab_source(plan, tab, i, s)
+                rank = tab[plan.rank + i * plan.G + jnp.maximum(a, 0)]
+                copies.append(
+                    pltpu.make_async_copy(
+                        near_hbm.at[low, half, :, i, rank], blocks.at[slot, i], near_sem.at[slot, i]
+                    )
+                )
+            return copies
+
+        def stores(s, slot):
+            copies = []
+            for c in range(STREAMS):
+                at = pl.ds(c * part, part)
+                copies.append(
+                    pltpu.make_async_copy(slab.at[slot, at], out_hbm.at[s, at], store_sem.at[slot, c])
+                )
+            return copies
+
+        def start(copies):
+            for copy in copies:
+                copy.start()
+
+        def wait(copies):
+            for copy in copies:
+                copy.wait()
+
+        start(loads(0, 0))
+        start(loads(1, 1))
+
+        def step(s, carry):
+            slot = lax.rem(s, 4)
+            ahead = lax.rem(s + 2, 4)
+
+            @pl.when(s + 2 < count)
+            def _():
+                @pl.when(s >= 2)
+                def _():
+                    wait(stores(s - 2, ahead))
+
+                start(loads(s + 2, ahead))
+
+            wait(loads(s, slot))
+            live = jnp.logical_not((s == 0) & (tab[plan.rho] < PT))
+            for i in range(2):
+                a, _, half = slab_source(plan, tab, i, s)
+
+                @pl.when(live & (a >= 0))
+                def _(i=i, half=half):
+                    add_blocks(
+                        plan, tab, i, s, half, slab.at[slot], lambda k, t: blocks[slot, i, k, t], slots
+                    )
+
+            start(stores(s, slot))
+            return carry
+
+        lax.fori_loop(0, count, step, 0)
+        for s in range(count - 4, count):
+            wait(stores(s, s % 4))
+
+    hbm = pl.BlockSpec(memory_space=pl.ANY)
     return pl.pallas_call(
         body,
         grid_spec=pltpu.PrefetchScalarGridSpec(
             num_scalar_prefetch=1,
-            grid=(total.shape[0],),
-            in_specs=[slab, near_spec(plan, 0), near_spec(plan, 1)],
-            out_specs=slab,
+            grid=(1,),
+            in_specs=[hbm, hbm],
+            out_specs=hbm,
+            scratch_shapes=[
+                pltpu.VMEM((4, rows, TILE), jnp.float32),
+                pltpu.VMEM((4, 2, R, plan.cap_l, TILE, TILE), jnp.bfloat16),
+                pltpu.SemaphoreType.DMA((4, STREAMS)),
+                pltpu.SemaphoreType.DMA((4, 2)),
+                pltpu.SemaphoreType.DMA((4, STREAMS)),
+            ],
         ),
         out_shape=jax.ShapeDtypeStruct(total.shape, jnp.float32),
         input_output_aliases={1: 0},
         compiler_params=pltpu.CompilerParams(vmem_limit_bytes=VMEM_LIMIT),
         name="add_near",
-    )(table, total, near, near)
+    )(table, total, near)
 
 
 def permute(x, plan, target):
@@ -482,15 +543,20 @@
     return factor, inverse
 
 
-def scaled_half(block, largest):
+def encode(blocks):
+    largest = jnp.max(jnp.abs(blocks), axis=1, keepdims=True)
     exponent = jnp.clip(jnp.ceil(jnp.log2(jnp.maximum(largest, 1e-30))), -100.0, 100.0)
-    scaled = (block * jnp.exp2(-exponent)).astype(jnp.float16)
-    return jnp.concatenate([scaled, jnp.full((16, TILE), exponent, jnp.float16)], axis=0)
-
-
-def from_half(parts):
-    exponent = parts[:, -1:, :1].astype(jnp.float32)
-    return parts[:, :-16].astype(jnp.float32) * jnp.exp2(exponent)
+    fixed = jnp.clip(jnp.round(blocks * jnp.exp2(15.0 - exponent)), -32767.0, 32767.0).astype(jnp.int32)
+    words = (fixed[:, : PD // 2] << 16) | (fixed[:, PD // 2 :] & 0xFFFF)
+    tail = jnp.broadcast_to(exponent.astype(jnp.int32), (blocks.shape[0], 8, TILE))
+    return jnp.concatenate([words, tail], axis=1)
+
+
+def decode(words):
+    scale = jnp.exp2((words[PD // 2 : PD // 2 + 1] - 15).astype(jnp.float32))
+    pairs = words[: PD // 2]
+    fixed = jnp.concatenate([pairs >> 16, (pairs << 16) >> 16], axis=0)
+    return fixed.astype(jnp.float32) * scale
 
 
 def on_device(front_blocks, child_updates, child_map):
@@ -501,9 +567,9 @@
     front = front_blocks.reshape(front_rows, tile * slots, tile)
     updates = jnp.transpose(child_updates, (0, 1, 3, 2, 4))
 
+    head = pack_panel(plan, table, updates)
     table, first = lax.optimization_barrier((table, front[0]))
     front_head = lax.all_gather(first, "row")
-    head = pack_panel(plan, table, updates)
     moved = lax.all_to_all(head, COL, 0, 0, tiled=True)
 
     def exchange(blocks, axes, count, after):
@@ -518,15 +584,13 @@
     child_head, near = lax.optimization_barrier((child_head, near))
     panel = assemble_panel(plan, table, front_head, child_head, slots)
     diag_tiles = lax.all_gather(panel[0], COL)
+    count = slots // R
+    piece = encode(lax.dynamic_slice_in_dim(panel, lax.axis_index("row") * count, count, axis=0))
+    piece = permute(piece, plan, lambda rho, h, kl: (kl, h, rho))
     diagonal = jnp.concatenate([diag_tiles[k] for k in range(PT)], axis=1)
-    count = slots // R
-    piece = lax.dynamic_slice_in_dim(panel, lax.axis_index("row") * count, count, axis=0)
-    piece = scaled_half(piece.reshape(count * PD, TILE), jnp.max(jnp.abs(panel)))
-    piece, far_in = lax.optimization_barrier((piece, far_in))
-    piece = permute(piece, plan, lambda rho, h, kl: (kl, h, rho))
-    row_half = lax.all_gather(piece, COL)
-    near_in = exchange(near, AXES, R * L, (row_half, diagonal))
-    row_panel = from_half(row_half).reshape(L * count, PD, TILE)
+    diagonal, piece = lax.optimization_barrier((diagonal, piece))
+    near_in = exchange(near, AXES, R * L, piece)
+    row_panel = lax.all_gather(piece, COL, tiled=True)
 
     factor, inverse = panel_factor(diagonal)
     col_parts = solve_blocks(inverse, panel, True)

time: 695 us -> 657 us (0.945)
  the two profiles are of different devices: /device:TPU:0 before, /device:TPU:5 now
where the time goes in v2:
time: 657 us; the launch traced here: 649 us
  waiting for transfers between devices  250 us (38%)
  Pallas kernels  197 us (30%)
  other arithmetic  125 us (19%)
  local copies, waits for them, and re-layouts  31.2 us (5%)
  starting transfers between devices  18.6 us (3%)
  between operations  16.6 us (3%)
  matrix products  11.1 us (2%)
    all_gather x1, waiting for transfers between devices, on_device(): child_head = lax.all_gather(moved, 'row')  90 us
    all_gather x1, waiting for transfers between devices, on_device(): row_panel = lax.all_gather(piece, COL, tiled=True)  84.1 us
    pallas_call x1, Pallas kernels, trailing(): pl.pallas_call(body, grid_spec=pltpu.PrefetchScalarGridSpec(num_scalar_pr...  79.2 us
    another operation x14, other arithmetic, panel_factor(): factor = jnp.linalg.cholesky(diagonal)  78.7 us
    all_gather x1, waiting for transfers between devices, on_device(): diag_tiles = lax.all_gather(panel[0], COL)  75 us
    another operation x4, other arithmetic, panel_factor(): lax.linalg.triangular_solve(factor, jnp.eye(PD, dtype=jnp.float32), left_...  41.4 us
    pallas_call x1, Pallas kernels, add_near(): pl.pallas_call(body, grid_spec=pltpu.PrefetchScalarGridSpec(num_scalar_pr...  31.2 us
    pallas_call x2, Pallas kernels, solve_blocks(): pl.pallas_call(body, grid=(count // pair,), in_specs=[whole, pl.BlockSpec...  23 us
  transfers between devices with their start and end apart: 8, of which 3 were waited for; matrix products, arithmetic and copies ran while one was open for 23% of the time, Pallas kernels for 26%

profile of v2, /device:TPU:5, one launch (start us, length us, event | category | flops | bytes accessed | tf_op | source)
XLA Modules:
  0.0 649.4 jit_solution(2243943739468381945)
XLA Ops:
  13.1 3.0 pack_panel.1
  16.1 5.8 all-to-all-start
  21.9 16.3 %pack_far_direct.1.held = bf16[4,4,2,2,3,2,128,128]{7,6,5,4,3,2,1,0:T(8,128)(2,1)} custom-call(s32[164]{0:T(256)S(1)} %concatenate.17.tab, bf16[2,24,12,128,128]{4,3,2,1,0:T(8,128)(2,1)} %bitcast.97), custom_call_target="tpu_custom_call" | custom-call | tf_op jit(solution)/shard_map/pack_far_direct/pallas_call | solution.py:159
  38.1 18.6 %pack_far_turned.1 = bf16[4,4,2,2,3,2,128,128]{7,6,5,4,3,2,1,0:T(8,128)(2,1)} custom-call(s32[164]{0:T(256)S(1)} %concatenate.17.tab, bf16[2,24,12,128,128]{4,3,2,1,0:T(8,128)(2,1)} %bitcast.98, bf16[4,4,2,2,3,2,128,128]{7,6,5,4,3,2,1,0:T(8,128)(2,1)} %pack_far_direct.1.held), custom_call_target="tpu_custom_call", output_to_operand_aliasing={{}: (2, {})} | custom-call | tf_op jit(solution)/shard_map/pack_far_turned/pallas_call | solution.py:173
  57.7 5.6 all-to-all-start.2
  64.1 18.5 %pack_near.1 = bf16[4,2,4,2,3,2,128,128]{7,6,5,4,3,2,1,0:T(8,128)(2,1)} custom-call(s32[164]{0:T(256)S(1)} %concatenate.17.tab, bf16[2,24,12,128,128]{4,3,2,1,0:T(8,128)(2,1)} %bitcast.99), custom_call_target="tpu_custom_call" | custom-call | tf_op jit(solution)/shard_map/pack_near/pallas_call | solution.py:100
  82.6 90.0 %all-gather.11.cloned.1.call-done = bf16[32,2,2,128,128]{4,3,2,1,0:T(8,128)(2,1)} async-done(((bf16[8,2,2,128,128]{4,3,2,1,0:T(8,128)(2,1)}), bf16[32,2,2,128,128]{4,3,2,1,0:T(8,128)(2,1)}) %all-gather.11.cloned.1.call-update) | async-done | bytes 4194320 | tf_op jit(solution)/shard_map/all_gather | solution.py:582
  172.6 7.1 %assemble_panel.1.x = f32[16,512,128]{2,1,0:T(8,128)S(1)} custom-call(s32[164]{0:T(256)S(1)} %concatenate.17.tab, f32[4,2048,128]{2,1,0:T(8,128)} %bitcast.106, bf16[4,8,2,2,128,128]{5,4,3,2,1,0:T(8,128)(2,1)} %bitcast.103, bf16[4,8,2,2,128,128]{5,4,3,2,1,0:T(8,128)(2,1)} %bitcast.104), custom_call_target="tpu_custom_call" | custom-call | tf_op jit(solution)/shard_map/assemble_panel/pallas_call | solution.py:261
  185.9 75.0 %all-gather.7.cloned.1.call-done = f32[8,512,128]{2,1,0:T(8,128)} async-done(((f32[1,512,128]{2,1,0:T(8,128)}), f32[8,512,128]{2,1,0:T(8,128)}) %all-gather.7.cloned.1.call-update) | async-done | bytes 2097168 | tf_op jit(solution)/shard_map/all_gather | solution.py:586
  263.6 6.3 all-to-all-start.1
  272.3 11.7 %cholesky.104 = f32[128,128]{1,0:T(8,128)S(1)} custom-call(f32[128,128]{1,0:T(8,128)S(1)} %cholesky.266), custom_call_target="Cholesky" | custom-call | tf_op jit(solution)/shard_map/jit(cholesky)/cholesky | solution.py:539
  284.0 9.8 %custom-call.30 = f32[1,128,128]{1,2,0:T(8,128)S(1)} custom-call(f32[1,128,128]{2,1,0:T(8,128)S(1)} %get-tuple-element.71), custom_call_target="InvertDiagBlocksLowerTriangular" | custom-call | tf_op jit(solution)/shard_map/jit(cholesky)/cholesky | solution.py:539
  296.5 11.7 %cholesky.217 = f32[128,128]{1,0:T(8,128)S(1)} custom-call(f32[128,128]{1,0:T(8,128)S(1)} %cholesky.270), custom_call_target="Cholesky" | custom-call | tf_op jit(solution)/shard_map/jit(cholesky)/cholesky | solution.py:539
  308.2 10.0 %custom-call.31 = f32[1,128,128]{1,2,0:T(8,128)S(1)} custom-call(f32[1,128,128]{2,1,0:T(8,128)S(1)} %get-tuple-element.68), custom_call_target="InvertDiagBlocksLowerTriangular" | custom-call | tf_op jit(solution)/shard_map/jit(cholesky)/cholesky | solution.py:539
  319.8 11.7 %cholesky.238 = f32[128,128]{1,0:T(8,128)S(1)} custom-call(f32[128,128]{1,0:T(8,128)S(1)} %cholesky.275), custom_call_target="Cholesky" | custom-call | tf_op jit(solution)/shard_map/jit(cholesky)/cholesky | solution.py:539
  331.6 9.8 %custom-call.32 = f32[1,128,128]{1,2,0:T(8,128)S(1)} custom-call(f32[1,128,128]{2,1,0:T(8,128)S(1)} %get-tuple-element.65), custom_call_target="InvertDiagBlocksLowerTriangular" | custom-call | tf_op jit(solution)/shard_map/jit(cholesky)/cholesky | solution.py:539
  342.8 11.7 %cholesky.255 = f32[128,128]{1,0:T(8,128)S(1)} custom-call(f32[128,128]{1,0:T(8,128)S(1)} %convolution_subtract_fusion.5), custom_call_target="Cholesky" | custom-call | tf_op jit(solution)/shard_map/jit(cholesky)/cholesky | solution.py:539
  360.5 13.9 %while.1 = (s32[]{:T(128)}, f32[512,512]{1,0:T(8,128)}, s32[4,2]{0,1:T(2,128)S(1)}, f32[4,128,128]{2,1,0:T(8,128)}, s32[]{:T(128)}) while((s32[]{:T(128)}, f32[512,512]{1,0:T(8,128)}, s32[4,2]{0,1:T(2,128)S(1)}, f32[4,128,128]{2,1,0:T(8,128)}, s32[]{:T(128)}) %tuple.53), condition=%wide.while_cond, body=%wide.while_body.sunk | while | flops 2 | bytes 132205 | solution.py:540
  374.3 40.1 %custom-call.33 = f32[4,128,128]{1,2,0:T(8,128)S(1)} custom-call(f32[4,128,128]{2,1,0:T(8,128)} %get-tuple-element.40), custom_call_target="InvertDiagBlocksLowerTriangular" | custom-call | tf_op jit(solution)/shard_map/triangular_solve | solution.py:540
  420.3 7.7 %solve_blocks.3 = (bf16[512,2048]{1,0:T(8,128)(2,1)S(1)}, bf16[512,2048]{1,0:T(8,128)(2,1)S(1)}) custom-call(f32[512,512]{1,0:T(8,128)S(1)} %pad_maximum_fusion.1.inv, f32[16,512,128]{2,1,0:T(8,128)} %copy-done), custom_call_target="tpu_custom_call" | custom-call | tf_op jit(solution)/shard_map/solve_blocks/pallas_call | solution.py:312
  430.7 84.1 %all-gather.9.cloned.1.call-done.x = s32[32,264,128]{2,1,0:T(8,128)} async-done(((s32[4,264,128]{2,1,0:T(8,128)}), s32[32,264,128]{2,1,0:T(8,128)}) %all-gather.9.cloned.1.call-update) | async-done | bytes 4325392 | tf_op jit(solution)/shard_map/all_gather | solution.py:593
  514.8 15.3 %solve_blocks.2 = (bf16[32,512,128]{2,1,0:T(8,128)(2,1)S(1)}, bf16[32,512,128]{2,1,0:T(8,128)(2,1)}) custom-call(f32[512,512]{1,0:T(8,128)S(1)} %pad_maximum_fusion.1.inv, s32[32,264,128]{2,1,0:T(8,128)} %all-gather.9.cloned.1.call-done.x), custom_call_target="tpu_custom_call" | custom-call | tf_op jit(solution)/shard_map/solve_blocks/pallas_call | solution.py:312
  532.0 79.2 %trailing.1.t_hbm = f32[32,2048,128]{2,1,0:T(8,128)} custom-call(s32[164]{0:T(256)S(1)} %concatenate.17.tab, f32[32,2048,128]{2,1,0:T(8,128)} %bitcast.102, f32[512,512]{1,0:T(8,128)S(1)} %get-tuple-element.53.l_ref, bf16[32,512,128]{2,1,0:T(8,128)(2,1)} %copy-done.1, bf16[32,512,128]{2,1,0:T(8,128)(2,1)} %get-tuple-element.27.rl, ...), custom_call_target="tpu_custom_call" | custom-call | flops 25769803776 | bytes 67108864 | tf_op jit(solution)/shard_map/trailing/pallas_call | solution.py:416
  611.2 31.2 %add_near.1 = f32[32,2048,128]{2,1,0:T(8,128)} custom-call(s32[164]{0:T(256)S(1)} %concatenate.17.tab, f32[32,2048,128]{2,1,0:T(8,128)} %trailing.1.t_hbm, bf16[4,2,4,2,3,2,128,128]{7,6,5,4,3,2,1,0:T(8,128)(2,1)} %bitcast.15.near_hbm), custom_call_target="tpu_custom_call", output_to_operand_aliasing={{}: (1, {})} | custom-call | tf_op jit(solution)/shard_map/add_near/pallas_call | solution.py:505
  (123 shorter events, 52.7 us)
Async XLA Ops:
  6.5 50.2 %all-gather.13.cloned.1.call-start = ((), (), s32[]{:S(2)}) async-start(), calls=%async_computation.6 | async-start | bytes 5242880 | tf_op jit(solution)/shard_map/all_gather | solution.py:572
  16.1 40.6 %all-to-all-start = ((bf16[8,2,2,128,128]{4,3,2,1,0:T(8,128)(2,1)}), bf16[8,2,2,128,128]{4,3,2,1,0:T(8,128)(2,1)S(1)}, u32[]{:S(2)}, u32[]{:S(2)}) async-start(bf16[8,2,2,128,128]{4,3,2,1,0:T(8,128)(2,1)} %pack_panel.1), calls=%async_computation | async-start | bytes 2097152 | tf_op jit(solution)/shard_map/all_to_all | solution.py:573
  56.7 1.0 copy-start.6
  57.7 205.1 %all-to-all-start.2 = ((bf16[16,24,128,128]{3,2,1,0:T(8,128)(2,1)}), bf16[16,24,128,128]{3,2,1,0:T(8,128)(2,1)}, u32[]{:S(2)}, u32[]{:S(2)}) async-start(bf16[16,24,128,128]{3,2,1,0:T(8,128)(2,1)} %bitcast.100), calls=%async_computation.2 | async-start | bytes 25165824 | tf_op jit(solution)/shard_map/all_to_all | solution.py:577
  63.3 109.3 %all-gather.11.cloned.1.call-start = ((), (), s32[]{:S(2)}) async-start(), calls=%async_computation.5 | async-start | bytes 5242880 | tf_op jit(solution)/shard_map/all_gather | solution.py:582
  64.1 196.9 %all-gather.7.cloned.1.call-start = ((), (), s32[]{:S(2)}) async-start(), calls=%async_computation.3 | async-start | bytes 2359296 | tf_op jit(solution)/shard_map/all_gather | solution.py:586
  179.7 1.9 copy-start
  185.2 77.6 %collective-permute-start = (s32[4,264,128]{2,1,0:T(8,128)S(1)}, s32[4,264,128]{2,1,0:T(8,128)S(1)}, u32[]{:S(2)}, u32[]{:S(2)}) collective-permute-start(s32[4,264,128]{2,1,0:T(8,128)S(1)} %pad_add_fusion), channel_id=1, source_target_pairs={{0,0},{1,8},{2,16},{3,24},{4,4},{5,12},{6,20},{7,28},{8,1},{9,9},{... | collective-permute-start | bytes 1622024 | tf_op jit(solution)/shard_map/ppermute | solution.py:535
  262.8 0.8 copy-start.8
  263.6 347.5 %all-to-all-start.1 = ((bf16[32,12,128,128]{3,2,1,0:T(8,128)(2,1)}), bf16[32,12,128,128]{3,2,1,0:T(8,128)(2,1)}, u32[]{:S(2)}, u32[]{:S(2)}) async-start(bf16[32,12,128,128]{3,2,1,0:T(8,128)(2,1)} %bitcast.101), calls=%async_computation.1 | async-start | bytes 25165824 | tf_op jit(solution)/shard_map/all_to_all | solution.py:577
  269.9 244.8 %all-gather.9.cloned.1.call-start = ((), (), s32[]{:S(2)}) async-start(), calls=%async_computation.4 | async-start | bytes 4866048 | tf_op jit(solution)/shard_map/all_gather | solution.py:593
  271.3 1.0 copy-start.7
  428.0 1.3 copy-start.2
  429.3 1.3 copy-start.4
  514.7 17.2 %copy-start.3 = (bf16[512,2048]{1,0:T(8,128)(2,1)S(1)}, bf16[512,2048]{1,0:T(8,128)(2,1)}, u32[]{:S(2)}) copy-start(bf16[512,2048]{1,0:T(8,128)(2,1)} %copy-done.2) | copy-start | bytes 6291460
  514.7 17.2 %copy-start.5 = (bf16[512,2048]{1,0:T(8,128)(2,1)S(1)}, bf16[512,2048]{1,0:T(8,128)(2,1)}, u32[]{:S(2)}) copy-start(bf16[512,2048]{1,0:T(8,128)(2,1)} %copy-done.4) | copy-start | bytes 6291460
  530.0 1.9 copy-start.1
Sparse Core Ops, SparseCore 0:
  13.3 36.0 all-gather.12
  65.7 106.8 all-gather.10
  182.5 78.3 all-gather.6
  272.6 242.0 all-gather.8

commit v3 on v2

--- a/solution.py
+++ b/solution.py
@@ -359,7 +359,7 @@
 def trailing(plan, table, front, factor, row_parts, col_parts, far, slots):
     R, L = plan.R, plan.L
     count = front.shape[0]
-    per_lane = row_parts[0].shape[0] // 2
+    share = slots // R
 
     def body(tab, f_ref, l_ref, rh, rl, ch, cl, direct0, turned0, direct1, turned1, out):
         fr = pl.program_id(0)
@@ -407,7 +407,13 @@
             out[0, pl.ds(0, TILE, stride=slots), :] = x.T
 
     slab = pl.BlockSpec((1, TILE * slots, TILE), lambda fr, tab: (fr, 0, 0))
-    row_spec = pl.BlockSpec((1, PD, TILE), lambda fr, tab: (lax.rem(fr, 2) * per_lane + fr // 2, 0, 0))
+
+    def row_at(fr, tab):
+        cs = fr // 2
+        other = (lax.rem(fr, 2) != tab[plan.kap] // R).astype(jnp.int32)
+        return ((cs // share * 2 + other) * share + lax.rem(cs, share), 0, 0)
+
+    row_spec = pl.BlockSpec((1, PD, TILE), row_at)
     col_spec = pl.BlockSpec((PD, slots * TILE), lambda fr, tab: (0, 0))
     factor_spec = pl.BlockSpec(
         (TILE, TILE), lambda fr, tab: (jnp.minimum(tab[plan.rho], PT - 1), jnp.minimum(tab[plan.kap], PT - 1))
@@ -586,11 +592,16 @@
     diag_tiles = lax.all_gather(panel[0], COL)
     count = slots // R
     piece = encode(lax.dynamic_slice_in_dim(panel, lax.axis_index("row") * count, count, axis=0))
-    piece = permute(piece, plan, lambda rho, h, kl: (kl, h, rho))
+    piece = jnp.concatenate(
+        [
+            permute(piece, plan, lambda rho, h, kl: (kl, h, rho)),
+            permute(piece, plan, lambda rho, h, kl: (kl, 1 - h, rho)),
+        ]
+    )
     diagonal = jnp.concatenate([diag_tiles[k] for k in range(PT)], axis=1)
     diagonal, piece = lax.optimization_barrier((diagonal, piece))
     near_in = exchange(near, AXES, R * L, piece)
-    row_panel = lax.all_gather(piece, COL, tiled=True)
+    row_panel = lax.all_gather(piece, "lane", tiled=True)
 
     factor, inverse = panel_factor(diagonal)
     col_parts = solve_blocks(inverse, panel, True)

time: 657 us -> 609 us (0.927)
  the two profiles are of different devices: /device:TPU:5 before, /device:TPU:0 now
where the time goes in v3:
time: 609 us; the launch traced here: 599 us
  Pallas kernels  198 us (33%)
  waiting for transfers between devices  197 us (32%)
  other arithmetic  126 us (21%)
  local copies, waits for them, and re-layouts  30.4 us (5%)
  starting transfers between devices  20.1 us (3%)
  between operations  16.5 us (3%)
  matrix products  11.2 us (2%)
    all_gather x1, waiting for transfers between devices, on_device(): child_head = lax.all_gather(moved, 'row')  90.3 us
    pallas_call x1, Pallas kernels, trailing(): pl.pallas_call(body, grid_spec=pltpu.PrefetchScalarGridSpec(num_scalar_pr...  81.1 us
    another operation x14, other arithmetic, panel_factor(): factor = jnp.linalg.cholesky(diagonal)  78.7 us
    all_gather x1, waiting for transfers between devices, on_device(): diag_tiles = lax.all_gather(panel[0], COL)  55 us
    another operation x4, other arithmetic, panel_factor(): lax.linalg.triangular_solve(factor, jnp.eye(PD, dtype=jnp.float32), left_...  41.4 us
    pallas_call x1, Pallas kernels, add_near(): pl.pallas_call(body, grid_spec=pltpu.PrefetchScalarGridSpec(num_scalar_pr...  32.1 us
    ppermute x2, waiting for transfers between devices, permute(): return lax.ppermute(x, AXES, pairs)  25.4 us
    pallas_call x2, Pallas kernels, solve_blocks(): pl.pallas_call(body, grid=(count // pair,), in_specs=[whole, pl.BlockSpec...  22.9 us
  transfers between devices with their start and end apart: 9, of which 5 were waited for; matrix products, arithmetic and copies ran while one was open for 25% of the time, Pallas kernels for 28%

profile of v3, /device:TPU:0, one launch (start us, length us, event | category | flops | bytes accessed | tf_op | source)
XLA Modules:
  0.0 599.5 jit_solution(17952296923435698431)
XLA Ops:
  15.9 7.3 %all-to-all-start = ((bf16[8,2,2,128,128]{4,3,2,1,0:T(8,128)(2,1)}), bf16[8,2,2,128,128]{4,3,2,1,0:T(8,128)(2,1)S(1)}, u32[]{:S(2)}, u32[]{:S(2)}) async-start(bf16[8,2,2,128,128]{4,3,2,1,0:T(8,128)(2,1)} %pack_panel.1), calls=%async_computation | async-start | bytes 2097152 | tf_op jit(solution)/shard_map/all_to_all | solution.py:579
  23.2 16.2 %pack_far_direct.1.held = bf16[4,4,2,2,3,2,128,128]{7,6,5,4,3,2,1,0:T(8,128)(2,1)} custom-call(s32[164]{0:T(256)S(1)} %concatenate.20.tab, bf16[2,24,12,128,128]{4,3,2,1,0:T(8,128)(2,1)} %bitcast.97), custom_call_target="tpu_custom_call" | custom-call | tf_op jit(solution)/shard_map/pack_far_direct/pallas_call | solution.py:159
  39.4 18.3 %pack_far_turned.1 = bf16[4,4,2,2,3,2,128,128]{7,6,5,4,3,2,1,0:T(8,128)(2,1)} custom-call(s32[164]{0:T(256)S(1)} %concatenate.20.tab, bf16[2,24,12,128,128]{4,3,2,1,0:T(8,128)(2,1)} %bitcast.98, bf16[4,4,2,2,3,2,128,128]{7,6,5,4,3,2,1,0:T(8,128)(2,1)} %pack_far_direct.1.held), custom_call_target="tpu_custom_call", output_to_operand_aliasing={{}: (2, {})} | custom-call | tf_op jit(solution)/shard_map/pack_far_turned/pallas_call | solution.py:173
  58.6 5.0 all-to-all-start.2
  64.4 18.4 %pack_near.1 = bf16[4,2,4,2,3,2,128,128]{7,6,5,4,3,2,1,0:T(8,128)(2,1)} custom-call(s32[164]{0:T(256)S(1)} %concatenate.20.tab, bf16[2,24,12,128,128]{4,3,2,1,0:T(8,128)(2,1)} %bitcast.99), custom_call_target="tpu_custom_call" | custom-call | tf_op jit(solution)/shard_map/pack_near/pallas_call | solution.py:100
  82.8 90.3 %all-gather.11.cloned.1.call-done = bf16[32,2,2,128,128]{4,3,2,1,0:T(8,128)(2,1)} async-done(((bf16[8,2,2,128,128]{4,3,2,1,0:T(8,128)(2,1)}), bf16[32,2,2,128,128]{4,3,2,1,0:T(8,128)(2,1)}) %all-gather.11.cloned.1.call-update) | async-done | bytes 4194320 | tf_op jit(solution)/shard_map/all_gather | solution.py:588
  173.1 6.2 %assemble_panel.1.x = f32[16,512,128]{2,1,0:T(8,128)S(1)} custom-call(s32[164]{0:T(256)S(1)} %concatenate.20.tab, f32[4,2048,128]{2,1,0:T(8,128)} %bitcast.106, bf16[4,8,2,2,128,128]{5,4,3,2,1,0:T(8,128)(2,1)} %bitcast.103, bf16[4,8,2,2,128,128]{5,4,3,2,1,0:T(8,128)(2,1)} %bitcast.104), custom_call_target="tpu_custom_call" | custom-call | tf_op jit(solution)/shard_map/assemble_panel/pallas_call | solution.py:261
  188.5 25.4 %collective-permute-done.1 = s32[4,264,128]{2,1,0:T(8,128)S(1)} collective-permute-done((s32[4,264,128]{2,1,0:T(8,128)S(1)}, s32[4,264,128]{2,1,0:T(8,128)S(1)}, u32[]{:S(2)}, u32[]{:S(2)}) %collective-permute-start.1) | collective-permute-done | bytes 540704 | tf_op jit(solution)/shard_map/ppermute | solution.py:541
  215.0 55.0 %all-gather.7.cloned.1.call-done = f32[8,512,128]{2,1,0:T(8,128)} async-done(((f32[1,512,128]{2,1,0:T(8,128)}), f32[8,512,128]{2,1,0:T(8,128)}) %all-gather.7.cloned.1.call-update) | async-done | bytes 2097168 | tf_op jit(solution)/shard_map/all_gather | solution.py:592
  278.0 11.7 %cholesky.104 = f32[128,128]{1,0:T(8,128)S(1)} custom-call(f32[128,128]{1,0:T(8,128)S(1)} %cholesky.266), custom_call_target="Cholesky" | custom-call | tf_op jit(solution)/shard_map/jit(cholesky)/cholesky | solution.py:545
  289.7 9.8 %custom-call.30 = f32[1,128,128]{1,2,0:T(8,128)S(1)} custom-call(f32[1,128,128]{2,1,0:T(8,128)S(1)} %get-tuple-element.71), custom_call_target="InvertDiagBlocksLowerTriangular" | custom-call | tf_op jit(solution)/shard_map/jit(cholesky)/cholesky | solution.py:545
  302.2 11.7 %cholesky.217 = f32[128,128]{1,0:T(8,128)S(1)} custom-call(f32[128,128]{1,0:T(8,128)S(1)} %cholesky.270), custom_call_target="Cholesky" | custom-call | tf_op jit(solution)/shard_map/jit(cholesky)/cholesky | solution.py:545
  313.9 10.0 %custom-call.31 = f32[1,128,128]{1,2,0:T(8,128)S(1)} custom-call(f32[1,128,128]{2,1,0:T(8,128)S(1)} %get-tuple-element.68), custom_call_target="InvertDiagBlocksLowerTriangular" | custom-call | tf_op jit(solution)/shard_map/jit(cholesky)/cholesky | solution.py:545
  325.5 11.7 %cholesky.238 = f32[128,128]{1,0:T(8,128)S(1)} custom-call(f32[128,128]{1,0:T(8,128)S(1)} %cholesky.275), custom_call_target="Cholesky" | custom-call | tf_op jit(solution)/shard_map/jit(cholesky)/cholesky | solution.py:545
  337.3 9.8 %custom-call.32 = f32[1,128,128]{1,2,0:T(8,128)S(1)} custom-call(f32[1,128,128]{2,1,0:T(8,128)S(1)} %get-tuple-element.65), custom_call_target="InvertDiagBlocksLowerTriangular" | custom-call | tf_op jit(solution)/shard_map/jit(cholesky)/cholesky | solution.py:545
  348.5 11.7 %cholesky.255 = f32[128,128]{1,0:T(8,128)S(1)} custom-call(f32[128,128]{1,0:T(8,128)S(1)} %convolution_subtract_fusion.5), custom_call_target="Cholesky" | custom-call | tf_op jit(solution)/shard_map/jit(cholesky)/cholesky | solution.py:545
  366.2 13.9 %while.1 = (s32[]{:T(128)}, f32[512,512]{1,0:T(8,128)}, s32[4,2]{0,1:T(2,128)S(1)}, f32[4,128,128]{2,1,0:T(8,128)}, s32[]{:T(128)}) while((s32[]{:T(128)}, f32[512,512]{1,0:T(8,128)}, s32[4,2]{0,1:T(2,128)S(1)}, f32[4,128,128]{2,1,0:T(8,128)}, s32[]{:T(128)}) %tuple.53), condition=%wide.while_cond, body=%wide.while_body.sunk | while | flops 2 | bytes 132205 | solution.py:546
  380.0 40.1 %custom-call.33 = f32[4,128,128]{1,2,0:T(8,128)S(1)} custom-call(f32[4,128,128]{2,1,0:T(8,128)} %get-tuple-element.40), custom_call_target="InvertDiagBlocksLowerTriangular" | custom-call | tf_op jit(solution)/shard_map/triangular_solve | solution.py:546
  426.0 7.7 %solve_blocks.3 = (bf16[512,2048]{1,0:T(8,128)(2,1)S(1)}, bf16[512,2048]{1,0:T(8,128)(2,1)S(1)}) custom-call(f32[512,512]{1,0:T(8,128)S(1)} %pad_maximum_fusion.1.inv, f32[16,512,128]{2,1,0:T(8,128)} %copy-done), custom_call_target="tpu_custom_call" | custom-call | tf_op jit(solution)/shard_map/solve_blocks/pallas_call | solution.py:312
  436.4 12.9 %all-gather.9.cloned.1.call-done.x = s32[32,264,128]{2,1,0:T(8,128)} async-done(((s32[8,264,128]{2,1,0:T(8,128)}), s32[32,264,128]{2,1,0:T(8,128)}) %all-gather.9.cloned.1.call-update) | async-done | bytes 4325392 | tf_op jit(solution)/shard_map/all_gather | solution.py:604
  449.3 15.2 %solve_blocks.2 = (bf16[32,512,128]{2,1,0:T(8,128)(2,1)S(1)}, bf16[32,512,128]{2,1,0:T(8,128)(2,1)}) custom-call(f32[512,512]{1,0:T(8,128)S(1)} %pad_maximum_fusion.1.inv, s32[32,264,128]{2,1,0:T(8,128)} %all-gather.9.cloned.1.call-done.x), custom_call_target="tpu_custom_call" | custom-call | tf_op jit(solution)/shard_map/solve_blocks/pallas_call | solution.py:312
  466.5 81.1 %trailing.1.t_hbm = f32[32,2048,128]{2,1,0:T(8,128)} custom-call(s32[164]{0:T(256)S(1)} %concatenate.20.tab, f32[32,2048,128]{2,1,0:T(8,128)} %bitcast.102, f32[512,512]{1,0:T(8,128)S(1)} %get-tuple-element.53.l_ref, bf16[32,512,128]{2,1,0:T(8,128)(2,1)} %copy-done.1, bf16[32,512,128]{2,1,0:T(8,128)(2,1)} %get-tuple-element.27.rl, ...), custom_call_target="tpu_custom_call" | custom-call | flops 25769803776 | bytes 67108864 | tf_op jit(solution)/shard_map/trailing/pallas_call | solution.py:422
  547.6 12.8 %all-to-all-done.1 = bf16[32,12,128,128]{3,2,1,0:T(8,128)(2,1)} async-done(((bf16[32,12,128,128]{3,2,1,0:T(8,128)(2,1)}), bf16[32,12,128,128]{3,2,1,0:T(8,128)(2,1)}, u32[]{:S(2)}, u32[]{:S(2)}) %all-to-all-start.1) | async-done | bytes 12582944 | tf_op jit(solution)/shard_map/all_to_all | solution.py:583
  560.3 32.1 %add_near.1 = f32[32,2048,128]{2,1,0:T(8,128)} custom-call(s32[164]{0:T(256)S(1)} %concatenate.20.tab, f32[32,2048,128]{2,1,0:T(8,128)} %trailing.1.t_hbm, bf16[4,2,4,2,3,2,128,128]{7,6,5,4,3,2,1,0:T(8,128)(2,1)} %bitcast.15.near_hbm), custom_call_target="tpu_custom_call", output_to_operand_aliasing={{}: (1, {})} | custom-call | tf_op jit(solution)/shard_map/add_near/pallas_call | solution.py:511
  (124 shorter events, 62.4 us)
Async XLA Ops:
  6.5 51.1 %all-gather.13.cloned.1.call-start = ((), (), s32[]{:S(2)}) async-start(), calls=%async_computation.6 | async-start | bytes 5242880 | tf_op jit(solution)/shard_map/all_gather | solution.py:578
  15.9 41.7 %all-to-all-start = ((bf16[8,2,2,128,128]{4,3,2,1,0:T(8,128)(2,1)}), bf16[8,2,2,128,128]{4,3,2,1,0:T(8,128)(2,1)S(1)}, u32[]{:S(2)}, u32[]{:S(2)}) async-start(bf16[8,2,2,128,128]{4,3,2,1,0:T(8,128)(2,1)} %pack_panel.1), calls=%async_computation | async-start | bytes 2097152 | tf_op jit(solution)/shard_map/all_to_all | solution.py:579
  57.6 1.0 copy-start.6
  58.6 213.2 %all-to-all-start.2 = ((bf16[16,24,128,128]{3,2,1,0:T(8,128)(2,1)}), bf16[16,24,128,128]{3,2,1,0:T(8,128)(2,1)}, u32[]{:S(2)}, u32[]{:S(2)}) async-start(bf16[16,24,128,128]{3,2,1,0:T(8,128)(2,1)} %bitcast.100), calls=%async_computation.2 | async-start | bytes 25165824 | tf_op jit(solution)/shard_map/all_to_all | solution.py:583
  63.6 109.5 %all-gather.11.cloned.1.call-start = ((), (), s32[]{:S(2)}) async-start(), calls=%async_computation.5 | async-start | bytes 5242880 | tf_op jit(solution)/shard_map/all_gather | solution.py:588
  64.4 205.6 %all-gather.7.cloned.1.call-start = ((), (), s32[]{:S(2)}) async-start(), calls=%async_computation.3 | async-start | bytes 2359296 | tf_op jit(solution)/shard_map/all_gather | solution.py:592
  179.4 1.9 copy-start
  184.8 29.0 %collective-permute-start.1 = (s32[4,264,128]{2,1,0:T(8,128)S(1)}, s32[4,264,128]{2,1,0:T(8,128)S(1)}, u32[]{:S(2)}, u32[]{:S(2)}) collective-permute-start(s32[4,264,128]{2,1,0:T(8,128)S(1)} %pad_add_fusion.1), channel_id=1, source_target_pairs={{0,4},{1,12},{2,20},{3,28},{4,0},{5,8},{6,16},{7,24},{8,5},{9,13},... | collective-permute-start | bytes 1622024 | tf_op jit(solution)/shard_map/ppermute | solution.py:541
  187.8 26.1 %collective-permute-start = (s32[4,264,128]{2,1,0:T(8,128)S(1)}, s32[4,264,128]{2,1,0:T(8,128)S(1)}, u32[]{:S(2)}, u32[]{:S(2)}) collective-permute-start(s32[4,264,128]{2,1,0:T(8,128)S(1)} %pad_add_fusion.1), channel_id=1, source_target_pairs={{0,0},{1,8},{2,16},{3,24},{4,4},{5,12},{6,20},{7,28},{8,1},{9,9},{... | collective-permute-start | bytes 1622024 | tf_op jit(solution)/shard_map/ppermute | solution.py:541
  271.9 288.5 %all-to-all-start.1 = ((bf16[32,12,128,128]{3,2,1,0:T(8,128)(2,1)}), bf16[32,12,128,128]{3,2,1,0:T(8,128)(2,1)}, u32[]{:S(2)}, u32[]{:S(2)}) async-start(bf16[32,12,128,128]{3,2,1,0:T(8,128)(2,1)} %bitcast.101), calls=%async_computation.1 | async-start | bytes 25165824 | tf_op jit(solution)/shard_map/all_to_all | solution.py:583
  275.7 173.6 %all-gather.9.cloned.1.call-start = ((), (), s32[]{:S(2)}) async-start(), calls=%async_computation.4 | async-start | bytes 5406720 | tf_op jit(solution)/shard_map/all_gather | solution.py:604
  277.0 1.0 copy-start.7
  433.7 1.3 copy-start.2
  435.0 1.3 copy-start.4
  449.3 17.2 %copy-start.3 = (bf16[512,2048]{1,0:T(8,128)(2,1)S(1)}, bf16[512,2048]{1,0:T(8,128)(2,1)}, u32[]{:S(2)}) copy-start(bf16[512,2048]{1,0:T(8,128)(2,1)} %copy-done.2) | copy-start | bytes 6291460
  449.3 17.2 %copy-start.5 = (bf16[512,2048]{1,0:T(8,128)(2,1)S(1)}, bf16[512,2048]{1,0:T(8,128)(2,1)}, u32[]{:S(2)}) copy-start(bf16[512,2048]{1,0:T(8,128)(2,1)} %copy-done.4) | copy-start | bytes 6291460
  464.5 1.9 copy-start.1
Sparse Core Ops, SparseCore 0:
  13.3 37.1 all-gather.12
  66.0 107.0 all-gather.10
  182.2 87.7 all-gather.6
  277.8 171.4 all-gather.8

commit v4 on v3

--- a/solution.py
+++ b/solution.py
@@ -589,7 +589,9 @@
     near = pack_near(plan, table, updates)
     child_head, near = lax.optimization_barrier((child_head, near))
     panel = assemble_panel(plan, table, front_head, child_head, slots)
-    diag_tiles = lax.all_gather(panel[0], COL)
+    first_tiles = permute(panel[0], plan, lambda rho, h, kl: (rho, 1 - h, kl))
+    first_tiles = jnp.where(lax.axis_index("half") == 0, panel[0], first_tiles)
+    diag_tiles = lax.all_gather(first_tiles, "lane")
     count = slots // R
     piece = encode(lax.dynamic_slice_in_dim(panel, lax.axis_index("row") * count, count, axis=0))
     piece = jnp.concatenate(

time: 609 us -> 603 us (level)
  waiting for transfers between devices: 197 us -> 180 us
  starting transfers between devices: 20.1 us -> 30.6 us
    all_gather x1, waiting for transfers between devices: 55 us -> 18.2 us  [on_device(): diag_tiles = lax.all_gather(first_tiles, 'lane')]
    ppermute x2 -> x3, waiting for transfers between devices: 25.4 us -> 44.2 us  [permute(): return lax.ppermute(x, AXES, pairs)]
    all_to_all x2, starting transfers between devices: 8.81 us -> 16.1 us  [exchange(): return lax.all_to_all(flat, axes, 0, 0, tiled=True).reshape(blocks.shape)]
  transfers between devices with their start and end apart: 9 -> 10, of which waited for: 5 -> 6; matrix products, arithmetic and copies ran while one was open for 25% -> 26% of each run, Pallas kernels for 28% -> 28%
where the time goes in v4:
time: 603 us; the launch traced here: 592 us
  Pallas kernels  197 us (33%)
  waiting for transfers between devices  180 us (30%)
  other arithmetic  127 us (21%)
  starting transfers between devices  30.6 us (5%)
  local copies, waits for them, and re-layouts  29.6 us (5%)
  between operations  16.6 us (3%)
  matrix products  11.2 us (2%)
    all_gather x1, waiting for transfers between devices, on_device(): child_head = lax.all_gather(moved, 'row')  90.5 us
    pallas_call x1, Pallas kernels, trailing(): pl.pallas_call(body, grid_spec=pltpu.PrefetchScalarGridSpec(num_scalar_pr...  80.3 us
    another operation x14, other arithmetic, panel_factor(): factor = jnp.linalg.cholesky(diagonal)  78.8 us
    ppermute x3, waiting for transfers between devices, permute(): return lax.ppermute(x, AXES, pairs)  44.2 us
    another operation x4, other arithmetic, panel_factor(): lax.linalg.triangular_solve(factor, jnp.eye(PD, dtype=jnp.float32), left_...  41.4 us
    pallas_call x1, Pallas kernels, add_near(): pl.pallas_call(body, grid_spec=pltpu.PrefetchScalarGridSpec(num_scalar_pr...  31.9 us
    pallas_call x2, Pallas kernels, solve_blocks(): pl.pallas_call(body, grid=(count // pair,), in_specs=[whole, pl.BlockSpec...  22.9 us
    pallas_call x1, Pallas kernels, pack_near(): pl.pallas_call(body, grid_spec=pltpu.PrefetchScalarGridSpec(num_scalar_pr...  18.3 us
  transfers between devices with their start and end apart: 10, of which 6 were waited for; matrix products, arithmetic and copies ran while one was open for 26% of the time, Pallas kernels for 28%

profile of v4, /device:TPU:0, one launch (start us, length us, event | category | flops | bytes accessed | tf_op | source)
XLA Modules:
  0.0 591.8 jit_solution(18412777757588364116)
XLA Ops:
  16.1 7.3 %all-to-all-start = ((bf16[8,2,2,128,128]{4,3,2,1,0:T(8,128)(2,1)}), bf16[8,2,2,128,128]{4,3,2,1,0:T(8,128)(2,1)S(1)}, u32[]{:S(2)}, u32[]{:S(2)}) async-start(bf16[8,2,2,128,128]{4,3,2,1,0:T(8,128)(2,1)} %pack_panel.1), calls=%async_computation | async-start | bytes 2097152 | tf_op jit(solution)/shard_map/all_to_all | solution.py:579
  23.4 16.0 %pack_far_direct.1.held = bf16[4,4,2,2,3,2,128,128]{7,6,5,4,3,2,1,0:T(8,128)(2,1)} custom-call(s32[164]{0:T(256)S(1)} %concatenate.20.tab, bf16[2,24,12,128,128]{4,3,2,1,0:T(8,128)(2,1)} %bitcast.95), custom_call_target="tpu_custom_call" | custom-call | tf_op jit(solution)/shard_map/pack_far_direct/pallas_call | solution.py:159
  39.4 17.8 %pack_far_turned.1 = bf16[4,4,2,2,3,2,128,128]{7,6,5,4,3,2,1,0:T(8,128)(2,1)} custom-call(s32[164]{0:T(256)S(1)} %concatenate.20.tab, bf16[2,24,12,128,128]{4,3,2,1,0:T(8,128)(2,1)} %bitcast.96, bf16[4,4,2,2,3,2,128,128]{7,6,5,4,3,2,1,0:T(8,128)(2,1)} %pack_far_direct.1.held), custom_call_target="tpu_custom_call", output_to_operand_aliasing={{}: (2, {})} | custom-call | tf_op jit(solution)/shard_map/pack_far_turned/pallas_call | solution.py:173
  64.3 18.3 %pack_near.1 = bf16[4,2,4,2,3,2,128,128]{7,6,5,4,3,2,1,0:T(8,128)(2,1)} custom-call(s32[164]{0:T(256)S(1)} %concatenate.20.tab, bf16[2,24,12,128,128]{4,3,2,1,0:T(8,128)(2,1)} %bitcast.97), custom_call_target="tpu_custom_call" | custom-call | tf_op jit(solution)/shard_map/pack_near/pallas_call | solution.py:100
  82.6 90.5 %all-gather.10.cloned.1.call-done = bf16[32,2,2,128,128]{4,3,2,1,0:T(8,128)(2,1)} async-done(((bf16[8,2,2,128,128]{4,3,2,1,0:T(8,128)(2,1)}), bf16[32,2,2,128,128]{4,3,2,1,0:T(8,128)(2,1)}) %all-gather.10.cloned.1.call-update) | async-done | bytes 4194320 | tf_op jit(solution)/shard_map/all_gather | solution.py:588
  185.0 20.2 %collective-permute-done = f32[512,128]{0,1:T(8,128)S(1)} collective-permute-done((f32[512,128]{0,1:T(8,128)S(1)}, f32[512,128]{0,1:T(8,128)S(1)}, u32[]{:S(2)}, u32[]{:S(2)}) %collective-permute-start) | collective-permute-done | bytes 262176 | tf_op jit(solution)/shard_map/ppermute | solution.py:541
  212.9 24.0 %collective-permute-done.2 = s32[4,264,128]{2,1,0:T(8,128)S(1)} collective-permute-done((s32[4,264,128]{2,1,0:T(8,128)S(1)}, s32[4,264,128]{2,1,0:T(8,128)S(1)}, u32[]{:S(2)}, u32[]{:S(2)}) %collective-permute-start.2) | collective-permute-done | bytes 540704 | tf_op jit(solution)/shard_map/ppermute | solution.py:541
  237.9 18.2 %all-gather.14.cloned.1.call-done = f32[2048,128]{0,1:T(8,128)} async-done(((f32[512,128]{0,1:T(8,128)}), f32[2048,128]{0,1:T(8,128)}) %all-gather.14.cloned.1.call-update) | async-done | bytes 1048592 | tf_op jit(solution)/shard_map/all_gather | solution.py:594
  257.5 10.8 %all-to-all-start.1 = ((bf16[32,12,128,128]{3,2,1,0:T(8,128)(2,1)}), bf16[32,12,128,128]{3,2,1,0:T(8,128)(2,1)}, u32[]{:S(2)}, u32[]{:S(2)}) async-start(bf16[32,12,128,128]{3,2,1,0:T(8,128)(2,1)} %bitcast.99), calls=%async_computation.1 | async-start | bytes 25165824 | tf_op jit(solution)/shard_map/all_to_all | solution.py:583
  270.6 11.7 %cholesky.104 = f32[128,128]{1,0:T(8,128)S(1)} custom-call(f32[128,128]{1,0:T(8,128)S(1)} %cholesky.266), custom_call_target="Cholesky" | custom-call | tf_op jit(solution)/shard_map/jit(cholesky)/cholesky | solution.py:545
  282.4 9.8 %custom-call.30 = f32[1,128,128]{1,2,0:T(8,128)S(1)} custom-call(f32[1,128,128]{2,1,0:T(8,128)S(1)} %get-tuple-element.71), custom_call_target="InvertDiagBlocksLowerTriangular" | custom-call | tf_op jit(solution)/shard_map/jit(cholesky)/cholesky | solution.py:545
  294.9 11.7 %cholesky.217 = f32[128,128]{1,0:T(8,128)S(1)} custom-call(f32[128,128]{1,0:T(8,128)S(1)} %cholesky.270), custom_call_target="Cholesky" | custom-call | tf_op jit(solution)/shard_map/jit(cholesky)/cholesky | solution.py:545
  306.6 10.0 %custom-call.31 = f32[1,128,128]{1,2,0:T(8,128)S(1)} custom-call(f32[1,128,128]{2,1,0:T(8,128)S(1)} %get-tuple-element.68), custom_call_target="InvertDiagBlocksLowerTriangular" | custom-call | tf_op jit(solution)/shard_map/jit(cholesky)/cholesky | solution.py:545
  318.2 11.7 %cholesky.238 = f32[128,128]{1,0:T(8,128)S(1)} custom-call(f32[128,128]{1,0:T(8,128)S(1)} %cholesky.275), custom_call_target="Cholesky" | custom-call | tf_op jit(solution)/shard_map/jit(cholesky)/cholesky | solution.py:545
  329.9 9.8 %custom-call.32 = f32[1,128,128]{1,2,0:T(8,128)S(1)} custom-call(f32[1,128,128]{2,1,0:T(8,128)S(1)} %get-tuple-element.65), custom_call_target="InvertDiagBlocksLowerTriangular" | custom-call | tf_op jit(solution)/shard_map/jit(cholesky)/cholesky | solution.py:545
  341.2 11.7 %cholesky.255 = f32[128,128]{1,0:T(8,128)S(1)} custom-call(f32[128,128]{1,0:T(8,128)S(1)} %convolution_subtract_fusion.5), custom_call_target="Cholesky" | custom-call | tf_op jit(solution)/shard_map/jit(cholesky)/cholesky | solution.py:545
  359.1 14.2 %while.1 = (s32[]{:T(128)}, f32[512,512]{1,0:T(8,128)}, s32[4,2]{0,1:T(2,128)S(1)}, f32[4,128,128]{2,1,0:T(8,128)}, s32[]{:T(128)}) while((s32[]{:T(128)}, f32[512,512]{1,0:T(8,128)}, s32[4,2]{0,1:T(2,128)S(1)}, f32[4,128,128]{2,1,0:T(8,128)}, s32[]{:T(128)}) %tuple.53), condition=%wide.while_cond, body=%wide.while_body.sunk | while | flops 2 | bytes 132205 | solution.py:546
  373.2 40.1 %custom-call.33 = f32[4,128,128]{1,2,0:T(8,128)S(1)} custom-call(f32[4,128,128]{2,1,0:T(8,128)} %get-tuple-element.40), custom_call_target="InvertDiagBlocksLowerTriangular" | custom-call | tf_op jit(solution)/shard_map/triangular_solve | solution.py:546
  419.2 7.7 %solve_blocks.3 = (bf16[512,2048]{1,0:T(8,128)(2,1)S(1)}, bf16[512,2048]{1,0:T(8,128)(2,1)S(1)}) custom-call(f32[512,512]{1,0:T(8,128)S(1)} %pad_maximum_fusion.1.inv, f32[16,512,128]{2,1,0:T(8,128)} %copy-done), custom_call_target="tpu_custom_call" | custom-call | tf_op jit(solution)/shard_map/solve_blocks/pallas_call | solution.py:312
  429.5 12.0 %all-gather.8.cloned.1.call-done.x = s32[32,264,128]{2,1,0:T(8,128)} async-done(((s32[8,264,128]{2,1,0:T(8,128)}), s32[32,264,128]{2,1,0:T(8,128)}) %all-gather.8.cloned.1.call-update) | async-done | bytes 4325392 | tf_op jit(solution)/shard_map/all_gather | solution.py:606
  441.6 15.3 %solve_blocks.2 = (bf16[32,512,128]{2,1,0:T(8,128)(2,1)S(1)}, bf16[32,512,128]{2,1,0:T(8,128)(2,1)}) custom-call(f32[512,512]{1,0:T(8,128)S(1)} %pad_maximum_fusion.1.inv, s32[32,264,128]{2,1,0:T(8,128)} %all-gather.8.cloned.1.call-done.x), custom_call_target="tpu_custom_call" | custom-call | tf_op jit(solution)/shard_map/solve_blocks/pallas_call | solution.py:312
  458.8 80.3 %trailing.1.t_hbm = f32[32,2048,128]{2,1,0:T(8,128)} custom-call(s32[164]{0:T(256)S(1)} %concatenate.20.tab, f32[32,2048,128]{2,1,0:T(8,128)} %bitcast.100, f32[512,512]{1,0:T(8,128)S(1)} %get-tuple-element.53.l_ref, bf16[32,512,128]{2,1,0:T(8,128)(2,1)} %copy-done.1, bf16[32,512,128]{2,1,0:T(8,128)(2,1)} %get-tuple-element.27.rl, ...), custom_call_target="tpu_custom_call" | custom-call | flops 25769803776 | bytes 67108864 | tf_op jit(solution)/shard_map/trailing/pallas_call | solution.py:422
  539.0 13.9 %all-to-all-done.1 = bf16[32,12,128,128]{3,2,1,0:T(8,128)(2,1)} async-done(((bf16[32,12,128,128]{3,2,1,0:T(8,128)(2,1)}), bf16[32,12,128,128]{3,2,1,0:T(8,128)(2,1)}, u32[]{:S(2)}, u32[]{:S(2)}) %all-to-all-start.1) | async-done | bytes 12582944 | tf_op jit(solution)/shard_map/all_to_all | solution.py:583
  552.9 31.9 %add_near.1 = f32[32,2048,128]{2,1,0:T(8,128)} custom-call(s32[164]{0:T(256)S(1)} %concatenate.20.tab, f32[32,2048,128]{2,1,0:T(8,128)} %trailing.1.t_hbm, bf16[4,2,4,2,3,2,128,128]{7,6,5,4,3,2,1,0:T(8,128)(2,1)} %bitcast.12.near_hbm), custom_call_target="tpu_custom_call", output_to_operand_aliasing={{}: (1, {})} | custom-call | tf_op jit(solution)/shard_map/add_near/pallas_call | solution.py:511
  (124 shorter events, 74.5 us)
Async XLA Ops:
  6.5 50.7 %all-gather.12.cloned.1.call-start = ((), (), s32[]{:S(2)}) async-start(), calls=%async_computation.5 | async-start | bytes 5242880 | tf_op jit(solution)/shard_map/all_gather | solution.py:578
  16.1 41.1 %all-to-all-start = ((bf16[8,2,2,128,128]{4,3,2,1,0:T(8,128)(2,1)}), bf16[8,2,2,128,128]{4,3,2,1,0:T(8,128)(2,1)S(1)}, u32[]{:S(2)}, u32[]{:S(2)}) async-start(bf16[8,2,2,128,128]{4,3,2,1,0:T(8,128)(2,1)} %pack_panel.1), calls=%async_computation | async-start | bytes 2097152 | tf_op jit(solution)/shard_map/all_to_all | solution.py:579
  57.2 1.0 copy-start.6
  58.2 199.4 %all-to-all-start.2 = ((bf16[16,24,128,128]{3,2,1,0:T(8,128)(2,1)}), bf16[16,24,128,128]{3,2,1,0:T(8,128)(2,1)}, u32[]{:S(2)}, u32[]{:S(2)}) async-start(bf16[16,24,128,128]{3,2,1,0:T(8,128)(2,1)} %bitcast.98), calls=%async_computation.2 | async-start | bytes 25165824 | tf_op jit(solution)/shard_map/all_to_all | solution.py:583
  63.5 109.6 %all-gather.10.cloned.1.call-start = ((), (), s32[]{:S(2)}) async-start(), calls=%async_computation.4 | async-start | bytes 5242880 | tf_op jit(solution)/shard_map/all_gather | solution.py:588
  64.2 191.9 %all-gather.14.cloned.1.call-start = ((), (), s32[]{:S(2)}) async-start(), calls=%async_computation.6 | async-start | bytes 1310720 | tf_op jit(solution)/shard_map/all_gather | solution.py:594
  180.2 1.9 copy-start
  182.3 22.8 %collective-permute-start = (f32[512,128]{0,1:T(8,128)S(1)}, f32[512,128]{0,1:T(8,128)S(1)}, u32[]{:S(2)}, u32[]{:S(2)}) collective-permute-start(f32[512,128]{0,1:T(8,128)S(1)} %bitcast.105), channel_id=1, source_target_pairs={{0,4},{1,5},{2,6},{3,7},{4,0},{5,1},{6,2},{7,3},{8,12},{9,13},{10,... | collective-permute-start | bytes 786440 | tf_op jit(solution)/shard_map/ppermute | solution.py:541
  208.7 28.2 %collective-permute-start.2 = (s32[4,264,128]{2,1,0:T(8,128)S(1)}, s32[4,264,128]{2,1,0:T(8,128)S(1)}, u32[]{:S(2)}, u32[]{:S(2)}) collective-permute-start(s32[4,264,128]{2,1,0:T(8,128)S(1)} %pad_add_fusion.1), channel_id=1, source_target_pairs={{0,4},{1,12},{2,20},{3,28},{4,0},{5,8},{6,16},{7,24},{8,5},{9,13},... | collective-permute-start | bytes 1622024 | tf_op jit(solution)/shard_map/ppermute | solution.py:541
  212.2 24.7 %collective-permute-start.1 = (s32[4,264,128]{2,1,0:T(8,128)S(1)}, s32[4,264,128]{2,1,0:T(8,128)S(1)}, u32[]{:S(2)}, u32[]{:S(2)}) collective-permute-start(s32[4,264,128]{2,1,0:T(8,128)S(1)} %pad_add_fusion.1), channel_id=1, source_target_pairs={{0,0},{1,8},{2,16},{3,24},{4,4},{5,12},{6,20},{7,28},{8,1},{9,9},{... | collective-permute-start | bytes 1622024 | tf_op jit(solution)/shard_map/ppermute | solution.py:541
  257.5 295.4 %all-to-all-start.1 = ((bf16[32,12,128,128]{3,2,1,0:T(8,128)(2,1)}), bf16[32,12,128,128]{3,2,1,0:T(8,128)(2,1)}, u32[]{:S(2)}, u32[]{:S(2)}) async-start(bf16[32,12,128,128]{3,2,1,0:T(8,128)(2,1)} %bitcast.99), calls=%async_computation.1 | async-start | bytes 25165824 | tf_op jit(solution)/shard_map/all_to_all | solution.py:583
  268.4 173.2 %all-gather.8.cloned.1.call-start = ((), (), s32[]{:S(2)}) async-start(), calls=%async_computation.3 | async-start | bytes 5406720 | tf_op jit(solution)/shard_map/all_gather | solution.py:606
  269.6 1.0 copy-start.7
  426.8 1.3 copy-start.2
  428.2 1.3 copy-start.4
  441.5 17.2 %copy-start.3 = (bf16[512,2048]{1,0:T(8,128)(2,1)S(1)}, bf16[512,2048]{1,0:T(8,128)(2,1)}, u32[]{:S(2)}) copy-start(bf16[512,2048]{1,0:T(8,128)(2,1)} %copy-done.2) | copy-start | bytes 6291460
  441.5 17.2 %copy-start.5 = (bf16[512,2048]{1,0:T(8,128)(2,1)S(1)}, bf16[512,2048]{1,0:T(8,128)(2,1)}, u32[]{:S(2)}) copy-start(bf16[512,2048]{1,0:T(8,128)(2,1)} %copy-done.4) | copy-start | bytes 6291460
  456.8 1.9 copy-start.1
Sparse Core Ops, SparseCore 0:
  13.3 37.1 all-gather.11
  65.9 107.1 all-gather.9
  206.0 50.0 all-gather.13
  270.4 171.0 all-gather.7
